TPU v7x, 32 devices: a whole 2x2x4 slice. The times are simulated.
32 devices in a mesh: grp: 4 (over y, x), ffn: 8 (over z, core).
Axes of the slice: x: 2, y: 2, z: 4, core: 2. Of those that a mesh axis runs over, the one named last changes fastest.
Arguments:
- layer_input: bfloat16 [288, 5120], P(None, 'ffn')
- norm_gain: float32 [5120], P('ffn'), may hold values from 0.1 to 1.9
- qkv_weight: bfloat16 [3, 5120, 2560], P(None, 'ffn', 'grp'), may hold values from -0.078125 to 0.078125
- key_cache: bfloat16 [880, 128, 2560], P('ffn', None, 'grp'), may hold values from -256 to 256
- value_cache: bfloat16 [880, 128, 2560], P('ffn', None, 'grp'), may hold values from -4 to 4
- out_weight: bfloat16 [2560, 5120], P('grp', 'ffn'), may hold values from -0.125 to 0.125
- ffn_gain: float32 [5120], replicated, may hold values from 0.1 to 1.9
- gate_up_weight: bfloat16 [2, 5120, 13824], P(None, None, 'ffn'), may hold values from -0.078125 to 0.078125
- down_weight: bfloat16 [13824, 5120], P('ffn'), may hold values from -0.0625 to 0.0625
- span_offsets: int32 [2], replicated, may hold values from 0 to 16256, as said below
- decode_lengths: int32 [32], replicated, may hold values from 1 to 16383, as said below
- page_table: int32 [34, 128], replicated, may hold values from -1 to 879, as said below
Outputs:
- layer_output: bfloat16 [288, 5120], P('grp', 'ffn')
Inputs may be any that keep to these rules, and one draw needn't show every extreme that they name: `span_offsets`: the largest offset equals 16256. `decode_lengths`: one length equals 16383, the others are under 2048. `page_table`: row r holds page ids in its first ceil(n / 128) slots, where n is its prefix length plus its new tokens (128 for prefill, 1 for decode), and -1 in the others; no page id appears twice in the table.
All inputs are finite; a program needn't handle non-finite values.
Results may differ from a plain program's by a relative error of at most 0.025.
Values may be sent and summed in bfloat16 or wider, within the bound.
A program may use at most 320 MiB of HBM per device.

v0:
```python
import math

import jax
import jax.numpy as jnp
from jax import lax
from jax.sharding import PartitionSpec as P

D = 5120
HD = 128
PAGE = 128
SPAN = 128
PRE = 2
DEC = 32
MAXP = 128
TOKENS = 288


EPS = 1e-05
NEG = -1e30
EXACT = lax.Precision.HIGHEST


def merged(array, axis, join):
    gathered = jax.tree.map(
        lambda a, kind: lax.all_gather(a.astype(kind), axis),
        array,
        (jnp.bfloat16, jnp.bfloat16, jnp.bfloat16),
    )

    def take(source):
        return jax.tree.map(
            lambda a, own: lax.dynamic_index_in_dim(a, source, 0, False).astype(own.dtype),
            gathered,
            array,
        )

    return lax.fori_loop(
        1, lax.axis_size(axis), lambda source, state: join(state, take(source)), take(0)
    )


def rotate(values, positions):
    half_width = values.shape[-1] // 2
    frequency = jnp.exp(
        jnp.arange(half_width, dtype=jnp.float32) * (-2.0 * math.log(10000.0) / values.shape[-1])
    )
    angles = positions.astype(jnp.float32)[:, None] * frequency[None, :]
    cosine = jnp.cos(angles)[:, None, :]
    sine_table = jnp.sin(angles)[:, None, :]
    leading = values[..., :half_width]
    trailing = values[..., half_width:]
    return jnp.concatenate(
        [leading * cosine - trailing * sine_table, trailing * cosine + leading * sine_table],
        axis=-1,
    )


def token_positions(span_offsets, decode_lengths):
    within = jnp.arange(SPAN, dtype=jnp.int32)
    prefill = (span_offsets[:, None] + within[None, :]).reshape(PRE * SPAN)
    return jnp.concatenate([prefill, decode_lengths])


def finish_projection(summed, squares, positions, group_heads):
    inverse = lax.rsqrt(squares / D + EPS)[:, None]
    row_count = summed.shape[0]
    queries = rotate((summed[:, 0] * inverse).reshape(row_count, group_heads, HD), positions)
    fresh_keys = rotate((summed[:, 1] * inverse).reshape(row_count, group_heads, HD), positions)
    fresh_values = (summed[:, 2] * inverse).reshape(row_count, group_heads, HD)
    stacked = jnp.stack([queries, fresh_keys, fresh_values], axis=1).astype(jnp.bfloat16)
    return stacked.reshape(row_count, 3, group_heads * HD)


def combine_parts(earlier, later):
    maxima = jnp.maximum(earlier[0], later[0])
    factor_a = jnp.exp(earlier[0] - maxima)
    factor_b = jnp.exp(later[0] - maxima)
    totals = earlier[1] * factor_a + later[1] * factor_b
    summed = earlier[2] * factor_a[:, :, None] + later[2] * factor_b[:, :, None]
    return (maxima, totals, summed)


def shards(
    layer_input,
    norm_gain,
    qkv_weight,
    key_cache,
    value_cache,
    out_weight,
    ffn_gain,
    gate_up_weight,
    down_weight,
    span_offsets,
    decode_lengths,
    page_table,
):
    group_width = qkv_weight.shape[2]
    group_heads = group_width // HD
    request_count = PRE + DEC
    input_f32 = layer_input.astype(jnp.float32)
    scaled = (input_f32 * norm_gain[None, :]).astype(jnp.bfloat16)
    squares = jnp.sum(input_f32 * input_f32, axis=1)
    positions = token_positions(span_offsets, decode_lengths)
    partial_value = jnp.einsum(
        "td,kdc->tkc", scaled, qkv_weight, preferred_element_type=jnp.float32
    )
    summed, norms = (
        lax.psum(partial_value.astype(jnp.bfloat16), "ffn").astype(jnp.float32),
        lax.psum(squares.astype(jnp.bfloat16), "ffn").astype(jnp.float32),
    )
    fresh = finish_projection(summed, norms, positions, group_heads)
    all_queries = fresh[:, 0]
    new_keys = fresh[:, 1]
    new_values = fresh[:, 2]
    page_count = key_cache.shape[0]
    local_ids = lax.axis_index("ffn") * page_count + jnp.arange(page_count, dtype=jnp.int32)
    matches = page_table[None, :, :] == local_ids[:, None, None]
    owners = jnp.sum(
        jnp.where(matches, jnp.arange(request_count, dtype=jnp.int32)[None, :, None], 0),
        axis=(1, 2),
    )
    slots = jnp.sum(
        jnp.where(matches, jnp.arange(MAXP, dtype=jnp.int32)[None, None, :], 0), axis=(1, 2)
    )
    in_use = jnp.any(matches, axis=(1, 2))
    prefixes = jnp.concatenate([span_offsets, decode_lengths])
    starts = jnp.concatenate(
        [jnp.arange(PRE, dtype=jnp.int32) * SPAN, PRE * SPAN + jnp.arange(DEC, dtype=jnp.int32)]
    )
    key_offsets = jnp.arange(PAGE, dtype=jnp.int32)
    query_offsets = jnp.arange(SPAN, dtype=jnp.int32)
    score_scale = HD ** (-0.5)
    prefix_len = prefixes[owners]
    row_start = starts[owners]
    query_count = jnp.where(owners < PRE, SPAN, 1)
    key_positions = slots[:, None] * PAGE + key_offsets[None, :]
    key_rows = jnp.clip(row_start[:, None] + key_positions - prefix_len[:, None], 0, TOKENS - 1)
    earlier = (key_positions < prefix_len[:, None])[:, :, None]
    page_keys = jnp.where(earlier, key_cache, new_keys[key_rows]).reshape(
        page_count, PAGE, group_heads, HD
    )
    page_values = jnp.where(earlier, value_cache, new_values[key_rows]).reshape(
        page_count, PAGE, group_heads, HD
    )
    query_rows = jnp.clip(row_start[:, None] + query_offsets[None, :], 0, TOKENS - 1)
    query_live = in_use[:, None] & (query_offsets[None, :] < query_count[:, None])
    query_positions = prefix_len[:, None] + query_offsets[None, :]
    page_queries = all_queries[query_rows].reshape(page_count, SPAN, group_heads, HD)
    visible = ((key_positions[:, None, :] <= query_positions[:, :, None]) & query_live[:, :, None])[
        :, :, None, :
    ]
    scores = (
        jnp.einsum("pqhd,pkhd->pqhk", page_queries, page_keys, preferred_element_type=jnp.float32)
        * score_scale
    )
    capped = jnp.where(visible, scores, NEG)
    page_max = jnp.max(capped, axis=3)
    weights = jnp.where(visible, jnp.exp(capped - page_max[..., None]), 0.0)
    page_total = jnp.sum(weights, axis=3)
    page_sum = jnp.einsum(
        "pqhk,pkhd->pqhd",
        weights.astype(jnp.bfloat16),
        page_values,
        preferred_element_type=jnp.float32,
    )
    token_index = jnp.arange(TOKENS, dtype=jnp.int32)
    routing_bool = (query_rows[:, :, None] == token_index[None, None, :]) & query_live[:, :, None]
    routing = routing_bool.astype(jnp.float32)
    covered = jnp.any(routing_bool, axis=1)
    aligned_max = jnp.einsum("pqt,pqh->pth", routing, page_max, precision=EXACT)
    maxima = jnp.max(jnp.where(covered[:, :, None], aligned_max, NEG), axis=0)
    back_max = jnp.einsum("pqt,th->pqh", routing, maxima, precision=EXACT)
    factor = jnp.where(query_live[:, :, None], jnp.exp(page_max - back_max), 0.0)
    totals = jnp.einsum("pqt,pqh->th", routing, page_total * factor, precision=EXACT)
    summed_values = jnp.einsum(
        "pqt,pqhd->thd", routing, page_sum * factor[..., None], precision=EXACT
    )
    maxima, totals, summed_values = merged((maxima, totals, summed_values), "ffn", combine_parts)
    heads_out = (
        (summed_values / totals[:, :, None]).astype(jnp.bfloat16).reshape(TOKENS, group_width)
    )
    head_part = jnp.dot(heads_out, out_weight, preferred_element_type=jnp.float32)
    attended = lax.psum(head_part.astype(jnp.bfloat16), "grp").astype(jnp.float32)
    residual = (input_f32 + attended).astype(jnp.bfloat16)
    quarter = TOKENS // lax.axis_size("grp")
    own_block = lax.dynamic_slice_in_dim(residual, lax.axis_index("grp") * quarter, quarter, 0)
    block_rows = lax.all_gather(own_block, "ffn", axis=1, tiled=True)
    rows_f32 = block_rows.astype(jnp.float32)
    inverse = lax.rsqrt(jnp.sum(rows_f32 * rows_f32, axis=1) / D + EPS)[:, None]
    normed = (rows_f32 * inverse * ffn_gain[None, :]).astype(jnp.bfloat16)
    gate_up = jnp.einsum("td,kdf->ktf", normed, gate_up_weight, preferred_element_type=jnp.float32)
    hidden = (jax.nn.silu(gate_up[0]) * gate_up[1]).astype(jnp.bfloat16)
    down_terms = jnp.dot(hidden, down_weight, preferred_element_type=jnp.float32)
    summed_out = lax.psum_scatter(
        down_terms.astype(jnp.bfloat16), "ffn", scatter_dimension=1, tiled=True
    ).astype(jnp.float32)
    return (own_block.astype(jnp.float32) + summed_out).astype(jnp.bfloat16)


def solution(mesh):
    in_specs = (
        P(None, "ffn"),
        P("ffn"),
        P(None, "ffn", "grp"),
        P("ffn", None, "grp"),
        P("ffn", None, "grp"),
        P("grp", "ffn"),
        P(),
        P(None, None, "ffn"),
        P("ffn", None),
        P(),
        P(),
        P(),
    )
    out_specs = P("grp", "ffn")
    return jax.shard_map(shards, mesh=mesh, in_specs=in_specs, out_specs=out_specs, check_vma=False)
```

profile of v0, /device:TPU:0, one launch (start us, length us, event | category | flops | bytes accessed | tf_op | source)
XLA Modules:
  0.0 685.3 jit_solution(8709481704613267075)
XLA Ops:
  6.5 1.7 copy-done
  8.2 3.1 convolution_convert_fusion.1
  11.4 1.2 multiply_reduce_fusion
  12.6 1.2 fusion.32
  13.8 1.1 compare_reduce_fusion
  14.9 0.7 add_bitcast_fusion
  15.7 0.7 pad_add_fusion.1
  16.5 1.2 gather_fusion.1
  17.8 0.7 broadcast_compare_fusion
  18.6 1.2 gather_fusion
  20.1 18.7 %psum.22 = bf16[288]{0:T(512)(128)(2,1)S(1)} all-reduce(bf16[288]{0:T(512)(128)(2,1)S(1)} %multiply_reduce_fusion), channel_id=1, replica_groups=mesh['grp'=4,'ffn'=8] {'ffn'}, use_global_device_ids=true, to_apply=%region_6.7 | all-reduce | flops 288 | bytes 1152 | tf_op jit(solution)/shard_map/psum | solution.py:109
  38.8 0.7 add_convert_fusion.3
  39.5 1.1 multiply_cosine_fusion
  40.7 6.3 fusion.21
  47.0 23.3 %copy.64 = bf16[110,128,640]{1,2,0:T(8,128)(2,1)} copy(bf16[110,128,640]{2,1,0:T(8,128)(2,1)} %param.17) | data formatting | bytes 36044800 | tf_op args[3]
  70.3 23.2 %copy.71 = bf16[110,128,640]{1,2,0:T(8,128)(2,1)} copy(bf16[110,128,640]{2,1,0:T(8,128)(2,1)} %param.18) | data formatting | bytes 36044800 | tf_op args[4]
  93.6 5.5 compare_and_fusion
  99.1 1.2 fusion.87
  100.6 1.3 copy.62
  101.9 1.4 broadcast_multiply_fusion
  103.3 1.2 subtract_convert_fusion
  104.9 40.8 %gather_fusion.2 = bf16[14080,640]{1,0:T(8,128)(2,1)} fusion(bf16[288,640]{1,0:T(8,128)(2,1)S(1)} %copy.63, s32[14336]{0:T(1024)S(1)} %pad_clamp_fusion.1), kind=kCustom, calls=%fused_computation.2 | custom fusion | bytes 36101120 | tf_op jit(solution)/shard_map/gather | solution.py:139
  145.7 23.8 %copy.65 = bf16[110,128,640]{1,2,0:T(8,128)(2,1)} copy(bf16[110,128,640]{2,1,0:T(8,128)(2,1)} %bitcast.123) | data formatting | bytes 36044800 | tf_op jit(solution)/shard_map/gather | solution.py:139
  169.8 40.8 %gather_fusion.4 = bf16[14080,640]{1,0:T(8,128)(2,1)} fusion(bf16[288,640]{1,0:T(8,128)(2,1)S(1)} %fusion.72, s32[14336]{0:T(1024)S(1)} %pad_clamp_fusion.1), kind=kCustom, calls=%fused_computation.4 | custom fusion | bytes 36101120 | tf_op jit(solution)/shard_map/gather | solution.py:142
  210.7 22.9 %copy.72 = bf16[110,128,640]{1,2,0:T(8,128)(2,1)} copy(bf16[110,128,640]{2,1,0:T(8,128)(2,1)} %bitcast.122) | data formatting | bytes 36044800 | tf_op jit(solution)/shard_map/gather | solution.py:142
  233.8 40.8 %gather_fusion.3 = bf16[14080,640]{1,0:T(8,128)(2,1)} fusion(bf16[288,640]{1,0:T(8,128)(2,1)S(1)} %copy.67, s32[14336]{0:T(1024)S(1)} %pad_clamp_fusion), kind=kCustom, calls=%fused_computation.3 | custom fusion | bytes 36101120 | tf_op jit(solution)/shard_map/gather | solution.py:148
  274.6 39.4 %reshape.515 = bf16[110,128,5,128]{3,2,1,0:T(8,128)(2,1)} reshape(bf16[14080,640]{1,0:T(8,128)(2,1)} %gather_fusion.3) | data formatting | bytes 36044800 | tf_op jit(solution)/shard_map/reshape | solution.py:148
  314.0 36.2 %broadcast_select_fusion = (bf16[110,128,640]{1,2,0:T(8,128)(2,1)}, bf16[110,128,640]{1,2,0:T(8,128)(2,1)}) fusion(bf16[110,128,640]{1,2,0:T(8,128)(2,1)} %copy.71, bf16[110,128,640]{1,2,0:T(8,128)(2,1)} %copy.72, pred[110,128]{1,0:T(8,128)(4,1)S(1)} %copy-done.9, bf16[110,128,640]{1,2,0:T(8,128)(2,1)} %copy.64, bf16[110,128,640]{1,2,0:T(8,128)(2,1)} %copy.65), kind=kLoop, calls=%fused_computation.28 | loop fusion | flops 18022400 | bytes 108148480 | tf_op jit(solution)/shard_map/jit(_where)/select_n | solution.py:142
  350.2 32.5 %fusion.4 = (f32[110,128,5]{1,2,0:T(8,128)S(1)}, f32[110,5,128,128]{3,2,1,0:T(8,128)}) fusion(pred[110,128,128]{1,2,0:T(8,128)(4,1)S(1)} %copy-done.2, bf16[110,128,5,128]{1,3,2,0:T(8,128)(2,1)} %bitcast.121, bf16[110,128,5,128]{3,2,1,0:T(8,128)(2,1)} %reshape.515), kind=kOutput, calls=%fused_computation.19 | convolution fusion | flops 2333830400 | bytes 74173440 | tf_op jit(solution)/shard_map/pqhd,pkhd->pqhk/dot_general | solution.py:153
  382.8 23.8 %fusion.5 = (bf16[110,128,5,128]{1,3,2,0:T(8,128)(2,1)}, f32[110,128,5]{1,2,0:T(8,128)S(1)}) fusion(f32[110,5,128,128]{3,2,1,0:T(8,128)} %get-tuple-element.251, f32[110,128,5]{1,2,0:T(8,128)S(1)} %get-tuple-element.250, pred[110,128,128]{1,2,0:T(8,128)(4,1)S(1)} %copy-done.2), kind=kLoop, calls=%fused_computation.20 | loop fusion | flops 53996800 | bytes 56432640 | tf_op jit(solution)/shard_map/convert_element_type | solution.py:162
  406.6 8.3 %select_reduce_fusion = f32[288,5]{0,1:T(8,128)S(1)} fusion(f32[110,128,5]{1,2,0:T(8,128)S(1)} %get-tuple-element.250, s32[110,128]{1,0:T(8,128)S(1)} %copy-done.6, pred[110,128]{1,0:T(8,128)(4,1)S(1)} %copy-done.8, pred[110,288]{1,0:T(8,128)(4,1)S(1)} %copy-done.10), kind=kOutput, calls=%fused_computation.59 | convolution fusion | flops 251727840 | bytes 389440 | tf_op jit(solution)/shard_map/pqt,pqh->pth/dot_general | solution.py:170
  414.9 5.7 fusion.50
  420.7 26.0 %fusion.7 = f32[110,5,128,128]{3,2,0,1:T(8,128)} fusion(bf16[110,128,5,128]{1,3,2,0:T(8,128)(2,1)} %get-tuple-element.232, bf16[110,128,5,128]{1,3,2,0:T(8,128)(2,1)} %bitcast.124), kind=kOutput, calls=%fused_computation.22 | convolution fusion | flops 2306867200 | bytes 72089600 | tf_op jit(solution)/shard_map/pqhk,pkhd->pqhd/dot_general | solution.py:160
  446.7 49.1 %fusion.41 = bf16[288,5,128]{2,0,1:T(8,128)(2,1)} fusion(f32[110,5,128,128]{3,2,0,1:T(8,128)} %fusion.7, f32[110,128,5]{1,0,2:T(8,128)S(1)} %copy.75, s32[110,128]{1,0:T(8,128)S(1)} %copy-done.6, pred[110,128]{1,0:T(8,128)(4,1)S(1)} %copy-done.8), kind=kOutput, calls=%fused_computation.62 | convolution fusion | flops 31160012800 | bytes 36765440 | tf_op jit(solution)/shard_map/pqt,pqhd->thd/dot_general | solution.py:175
  496.1 7.5 %fusion.59 = bf16[1,288,5]{1,2,0:T(8,128)(2,1)S(1)} fusion(s32[110,128]{1,0:T(8,128)S(1)} %copy-done.6, pred[110,128]{1,0:T(8,128)(4,1)S(1)} %copy-done.8, f32[110,128,5]{1,2,0:T(8,128)S(1)} %get-tuple-element.233, f32[110,128,5]{1,2,0:T(8,128)S(1)} %fusion.50), kind=kOutput, calls=%fused_computation.69 | convolution fusion | flops 251484320 | bytes 636480 | tf_op jit(solution)/shard_map/pqt,pqh->th/dot_general | solution.py:174
  503.6 14.4 %all-gather.4 = bf16[8,288,5]{1,2,0:T(8,128)(2,1)S(1)} all-gather(bf16[1,288,5]{1,2,0:T(8,128)(2,1)S(1)} %fusion.59), channel_id=3, replica_groups=mesh['grp'=4,'ffn'=8] {'ffn'}, dimensions={0}, use_global_device_ids=true | all-gather | bytes 25920 | tf_op jit(solution)/shard_map/all_gather | solution.py:25
  518.0 14.1 %all-gather.3 = bf16[8,288,5]{1,2,0:T(8,128)(2,1)S(1)} all-gather(bf16[1,288,5]{1,2,0:T(8,128)(2,1)S(1)} %convert_bitcast_fusion), channel_id=2, replica_groups=mesh['grp'=4,'ffn'=8] {'ffn'}, dimensions={0}, use_global_device_ids=true | all-gather | bytes 25920 | tf_op jit(solution)/shard_map/all_gather | solution.py:25
  532.1 1.0 slice_convert_fusion
  533.1 0.5 copy.77
  533.6 20.5 %while.19 = (s32[]{:T(128)}, f32[288,5]{0,1:T(8,128)S(1)}, f32[288,5]{0,1:T(8,128)S(1)}, f32[288,5,128]{2,1,0:T(8,128)S(1)}, bf16[8,288,5]{1,2,0:T(8,128)(2,1)S(...) while((s32[]{:T(128)}, f32[288,5]{0,1:T(8,128)S(1)}, ...), condition=%wide.region_11.12_spmd, body=%wide.region_10.11_spmd.sunk | while | flops 748805 | bytes 2655511 | solution.py:37
  533.9 1.0 constant_dynamic-slice_fusion.2
  535.0 1.6 fusion.98
  536.9 1.0 constant_dynamic-slice_fusion.2
  537.9 1.6 fusion.98
  539.8 1.0 constant_dynamic-slice_fusion.2
  540.8 1.6 fusion.98
  542.7 1.0 constant_dynamic-slice_fusion.2
  543.8 1.6 fusion.98
  545.7 1.0 constant_dynamic-slice_fusion.2
  546.7 1.6 fusion.98
  548.6 1.0 constant_dynamic-slice_fusion.2
  549.6 1.6 fusion.98
  551.5 1.0 constant_dynamic-slice_fusion.2
  552.5 1.6 fusion.98
  555.0 1.3 convolution_convert_fusion.2
  556.5 42.8 %all-reduce.5.cloned.1.call-done = bf16[288,640]{1,0:T(8,128)(2,1)} async-done(((bf16[288,640]{1,0:T(8,128)(2,1)}), bf16[288,640]{1,0:T(8,128)(2,1)}) %all-reduce.5.cloned.1.call-update) | async-done | bytes 368656 | tf_op jit(solution)/shard_map/psum | solution.py:183
  599.2 0.9 fusion.77
  600.1 15.6 %all_gather.24 = bf16[72,5120]{1,0:T(8,128)(2,1)S(1)} all-gather(bf16[72,640]{1,0:T(8,128)(2,1)S(1)} %fusion.77), channel_id=1, replica_groups=mesh['grp'=4,'ffn'=8] {'ffn'}, dimensions={1}, use_global_device_ids=true | all-gather | bytes 829440 | tf_op jit(solution)/shard_map/all_gather | solution.py:187
  616.0 16.2 %convolution_bitcast_fusion = f32[2,72,1728]{2,1,0:T(8,128)S(1)} fusion(bf16[2,5120,1728]{1,2,0:T(8,128)(2,1)} %param.21, bf16[72,5120]{1,0:T(8,128)(2,1)S(1)} %all_gather.24, f32[5120]{0:T(1024)S(1)} %copy-done.11, f32[72]{0:T(128)S(1)} %add_rsqrt_fusion.1), kind=kOutput, calls=%fused_computation.50 | convolution fusion | flops 2549514240 | bytes 37142816 | tf_op jit(solution)/shard_map/td,kdf->ktf/dot_general | solution.py:191
  632.3 9.2 %convolution_convert_fusion = bf16[72,5120]{1,0:T(8,128)(2,1)S(1)} fusion(bf16[1728,5120]{1,0:T(8,128)(2,1)} %param.22, f32[2,72,1728]{2,1,0:T(8,128)S(1)} %convolution_bitcast_fusion), kind=kOutput, calls=%fused_computation.46 | convolution fusion | flops 1275134976 | bytes 19427328 | tf_op jit(solution)/shard_map/dot_general | solution.py:193
  641.5 1.4 copy.88
  643.0 33.8 %reduce-scatter.4.cloned.1.call-done = bf16[640,72]{1,0:T(8,128)(2,1)} async-done(((bf16[5120,72]{1,0:T(8,128)(2,1)}), bf16[640,72]{1,0:T(8,128)(2,1)}) %reduce-scatter.4.cloned.1.call-update) | async-done | bytes 92176
  676.8 1.0 copy.89
  677.9 0.7 add_convert_fusion.2
  (92 shorter events, 5.6 us)
Async XLA Ops:
  6.5 1.7 copy-start
  6.5 92.6 %all-reduce.3.cloned.1.call-start = ((), (), s32[]{:S(2)}) async-start(), calls=%async_computation.1 | async-start | bytes 2211840 | tf_op jit(solution)/shard_map/psum | solution.py:108
  11.3 520.8 %all-gather.7.cloned.1.call-start = ((), (), s32[]{:S(2)}) async-start(), calls=%async_computation.3 | async-start | bytes 3317760 | tf_op jit(solution)/shard_map/all_gather | solution.py:25
  20.1 50.3 %copy-start.5 = (s32[110,128]{1,0:T(8,128)}, s32[110,128]{1,0:T(8,128)S(1)}, u32[]{:S(2)}) copy-start(s32[110,128]{1,0:T(8,128)S(1)} %add_clamp_fusion) | copy-start | bytes 168964
  40.7 52.9 %copy-start.7 = (pred[110,128]{1,0:T(8,128)(4,1)}, pred[110,128]{1,0:T(8,128)(4,1)S(1)}, u32[]{:S(2)}) copy-start(pred[110,128]{1,0:T(8,128)(4,1)S(1)} %fusion.80) | copy-start | bytes 42244
  47.0 54.9 %copy-start.12 = (f32[288]{0:T(512)}, f32[288]{0:T(512)S(1)}, u32[]{:S(2)}) copy-start(f32[288]{0:T(512)S(1)} %add_rsqrt_fusion) | copy-start | bytes 3460
  145.7 23.8 %copy-start.3 = (bf16[288,3,640]{2,0,1:T(8,128)(2,1)S(1)}, bf16[288,3,640]{2,0,1:T(8,128)(2,1)}, u32[]{:S(2)}) copy-start(bf16[288,3,640]{2,0,1:T(8,128)(2,1)} %all-reduce.3.cloned.1.call-done) | copy-start | bytes 3317764
  145.7 24.0 %copy-start.13 = (f32[288]{0:T(512)S(1)}, f32[288]{0:T(512)}, u32[]{:S(2)}) copy-start(f32[288]{0:T(512)} %copy-done.12) | copy-start | bytes 3460
  274.6 39.4 %copy-start.9 = (pred[110,128]{1,0:T(8,128)(4,1)S(1)}, pred[110,128]{1,0:T(8,128)(4,1)}, u32[]{:S(2)}) copy-start(pred[110,128]{1,0:T(8,128)(4,1)} %broadcast_compare_fusion) | copy-start | bytes 42244
  314.0 36.3 %copy-start.2 = (pred[110,128,128]{1,2,0:T(8,128)(4,1)S(1)}, pred[110,128,128]{1,2,0:T(8,128)(4,1)}, u32[]{:S(2)}) copy-start(pred[110,128,128]{1,2,0:T(8,128)(4,1)} %compare_and_fusion) | copy-start | bytes 5406724
  382.8 23.9 %copy-start.6 = (s32[110,128]{1,0:T(8,128)S(1)}, s32[110,128]{1,0:T(8,128)}, u32[]{:S(2)}) copy-start(s32[110,128]{1,0:T(8,128)} %copy-done.5) | copy-start | bytes 168964
  382.8 23.9 %copy-start.8 = (pred[110,128]{1,0:T(8,128)(4,1)S(1)}, pred[110,128]{1,0:T(8,128)(4,1)}, u32[]{:S(2)}) copy-start(pred[110,128]{1,0:T(8,128)(4,1)} %copy-done.7) | copy-start | bytes 42244
  382.8 23.9 %copy-start.10 = (pred[110,288]{1,0:T(8,128)(4,1)S(1)}, pred[110,288]{1,0:T(8,128)(4,1)}, u32[]{:S(2)}) copy-start(pred[110,288]{1,0:T(8,128)(4,1)} %fusion.21) | copy-start | bytes 95044
  495.8 103.4 %all-reduce.5.cloned.1.call-start = ((), (), s32[]{:S(2)}) async-start(), calls=%async_computation.2 | async-start | bytes 737280 | tf_op jit(solution)/shard_map/psum | solution.py:183
  503.6 51.5 %copy-start.14 = (bf16[640,640]{1,0:T(8,128)(2,1)S(1)}, bf16[640,640]{1,0:T(8,128)(2,1)}, u32[]{:S(2)}) copy-start(bf16[640,640]{1,0:T(8,128)(2,1)} %param.19) | copy-start | bytes 2457604
  503.6 52.8 %copy-start.4 = (bf16[288,640]{1,0:T(8,128)(2,1)S(1)}, bf16[288,640]{1,0:T(8,128)(2,1)}, u32[]{:S(2)}) copy-start(bf16[288,640]{1,0:T(8,128)(2,1)} %param.14) | copy-start | bytes 1105924
  532.1 84.0 %copy-start.11 = (f32[5120]{0:T(1024)S(1)}, f32[5120]{0:T(1024)}, u32[]{:S(2)}) copy-start(f32[5120]{0:T(1024)} %param.20) | copy-start | bytes 61444
  556.3 120.5 %reduce-scatter.4.cloned.1.call-start = ((), (), s32[]{:S(2)}) async-start(), calls=%async_computation.4 | async-start | bytes 1474560
  616.0 62.5 %copy-start.1 = (bf16[3,640,640]{2,1,0:T(8,128)(2,1)S(1)}, bf16[3,640,640]{2,1,0:T(8,128)(2,1)}, u32[]{:S(2)}) copy-start(bf16[3,640,640]{2,1,0:T(8,128)(2,1)} %param.16) | copy-start | bytes 7372804
Sparse Core Ops, SparseCore 0:
  11.4 61.9 all-reduce.2
  496.0 36.0 all-gather.6
  556.5 42.7 all-reduce.4
  643.1 33.6 reduce-scatter.3
where the time goes:
time: 692 us; the launch traced here: 685 us
  local copies, waits for them, and re-layouts  275 us (40%)
  matrix products  159 us (23%)
  other arithmetic  97.3 us (14%)
  waiting for transfers between devices  76.7 us (11%)
  blocking collectives  62.8 us (9%)
  between operations  13.7 us (2%)
    gather x2, local copies, waits for them, and re-layouts, shards(): new_keys[key_rows]  64.7 us
    gather x2, local copies, waits for them, and re-layouts, shards(): new_values[key_rows]  63.7 us
    unnamed x34, local copies, waits for them, and re-layouts  50.8 us
    dot_general x1, matrix products, shards(): jnp.einsum('pqt,pqhd->thd', routing, page_sum * factor[..., None], precis...  49.1 us
    psum x1, waiting for transfers between devices, shards(): lax.psum(head_part.astype(jnp.bfloat16), 'grp').astype(jnp.float32)  42.8 us
    gather x1, local copies, waits for them, and re-layouts, shards(): all_queries[query_rows].reshape(page_count, SPAN, group_heads, HD)  40.8 us
    reshape x1, local copies, waits for them, and re-layouts, shards(): all_queries[query_rows].reshape(page_count, SPAN, group_heads, HD)  39.4 us
    select_n x1, other arithmetic, shards(): jnp.where(earlier, value_cache, new_values[key_rows])  36.2 us
  transfers between devices with their start and end apart: 4, of which 2 were waited for; matrix products, arithmetic and copies ran while one was open for 11% of the time, Pallas kernels for 0%

commit v1 on v0

v1 whole, which is shorter than its diff:
```python
import functools
import math

import jax
import jax.numpy as jnp
from jax import lax
from jax.experimental import pallas as pl
from jax.experimental.pallas import tpu as pltpu
from jax.sharding import PartitionSpec as P

D = 5120
HD = 128
PAGE = 128
SPAN = 128
PRE = 2
DEC = 32
MAXP = 128
TOKENS = 288


EPS = 1e-05
NEG = -1e30
SCALE = HD ** (-0.5)
GROUP = 4
SLOTS = 128
BUFFERS = 6
ROWS = 16


def rotate(values, positions):
    half_width = values.shape[-1] // 2
    frequency = jnp.exp(
        jnp.arange(half_width, dtype=jnp.float32) * (-2.0 * math.log(10000.0) / values.shape[-1])
    )
    angles = positions.astype(jnp.float32)[:, None] * frequency[None, :]
    cosine = jnp.cos(angles)[:, None, :]
    sine_table = jnp.sin(angles)[:, None, :]
    leading = values[..., :half_width]
    trailing = values[..., half_width:]
    return jnp.concatenate(
        [leading * cosine - trailing * sine_table, trailing * cosine + leading * sine_table],
        axis=-1,
    )


def token_positions(span_offsets, decode_lengths):
    within = jnp.arange(SPAN, dtype=jnp.int32)
    prefill = (span_offsets[:, None] + within[None, :]).reshape(PRE * SPAN)
    return jnp.concatenate([prefill, decode_lengths])


def finish_projection(summed, squares, positions, group_heads):
    inverse = lax.rsqrt(squares / D + EPS)[:, None]
    row_count = summed.shape[0]
    queries = rotate((summed[:, 0] * inverse).reshape(row_count, group_heads, HD), positions)
    fresh_keys = rotate((summed[:, 1] * inverse).reshape(row_count, group_heads, HD), positions)
    fresh_values = (summed[:, 2] * inverse).reshape(row_count, group_heads, HD)
    stacked = jnp.stack([queries, fresh_keys, fresh_values], axis=1).astype(jnp.bfloat16)
    return stacked.reshape(row_count, 3, group_heads * HD)


def split_bf16(value, pieces):
    out = []
    for _ in range(pieces):
        piece = value.astype(jnp.bfloat16).astype(jnp.float32)
        out.append(piece)
        value = value - piece
    return out


def attention_kernel(
    heads,
    plan,
    queries,
    new_keys,
    new_values,
    spread,
    start_m,
    start_l,
    start_o,
    key_cache,
    value_cache,
    packed,
    decode_out,
    decode_stats,
    key_buf,
    value_buf,
    run_m,
    run_l,
    run_o,
    dec_m,
    dec_l,
    dec_o,
    sems,
):
    end_first, end_prefill, end_all = plan[3, 0], plan[3, 1], plan[3, 2]

    def copies(group):
        place = lax.rem(group, BUFFERS)
        out = []
        for i in range(GROUP):
            page = plan[0, group * GROUP + i]
            out.append(
                pltpu.make_async_copy(
                    key_cache.at[page], key_buf.at[place, i], sems.at[place, 0, i]
                )
            )
            out.append(
                pltpu.make_async_copy(
                    value_cache.at[page], value_buf.at[place, i], sems.at[place, 1, i]
                )
            )
        return out

    def fetch(group):
        @pl.when(group < end_all)
        def _():
            for copy in copies(group):
                copy.start()

    for group in range(BUFFERS - 1):
        fetch(jnp.int32(group))

    run_m[...] = jnp.full_like(run_m, NEG)
    run_l[...] = jnp.zeros_like(run_l)
    run_o[...] = jnp.zeros_like(run_o)
    dec_m[...] = start_m[...]
    dec_l[...] = start_l[...]
    dec_o[...] = start_o[...]

    def prefill_step(request, head, keys, values, bias):
        columns = slice(head * HD, (head + 1) * HD)
        rows = pl.ds(pl.multiple_of(request * SPAN, SPAN), SPAN)
        scores = lax.dot_general(
            queries[rows, columns],
            keys,
            (((1,), (1,)), ((), ())),
            preferred_element_type=jnp.float32,
        )
        scores = scores + bias
        before = run_m[request, head]
        now = jnp.maximum(before, jnp.max(scores, axis=1, keepdims=True))
        fade = jnp.exp((before - now) * SCALE)
        weights = jnp.exp((scores - now[:, :1]) * SCALE)
        run_m[request, head] = now
        run_l[request, head] = run_l[request, head] * fade + jnp.sum(
            weights, axis=1, keepdims=True
        )
        run_o[request, head] = run_o[request, head] * fade + jnp.dot(
            weights.astype(jnp.bfloat16), values, preferred_element_type=jnp.float32
        )

    @pl.when(plan[3, 3] == 1)
    def _():
        causal = jnp.where(
            lax.broadcasted_iota(jnp.int32, (SPAN, SPAN), 1)
            <= lax.broadcasted_iota(jnp.int32, (SPAN, SPAN), 0),
            0.0,
            NEG,
        ).astype(jnp.float32)
        for request in range(PRE):
            rows = slice(request * SPAN, (request + 1) * SPAN)
            for head in range(heads):
                columns = slice(head * HD, (head + 1) * HD)
                prefill_step(
                    request, head, new_keys[rows, columns], new_values[rows, columns], causal
                )

    lanes = lax.broadcasted_iota(jnp.int32, (1, PAGE), 1)

    def prefill_group(group, place):
        request = (group >= end_first).astype(jnp.int32)
        bias = jnp.concatenate(
            [
                jnp.where(lanes < plan[1, group * GROUP + i], 0.0, NEG).astype(jnp.float32)
                for i in range(GROUP)
            ],
            axis=1,
        )
        for head in range(heads):
            columns = slice(head * HD, (head + 1) * HD)
            keys = key_buf[place, :, :, columns].reshape(GROUP * PAGE, HD)
            values = value_buf[place, :, :, columns].reshape(GROUP * PAGE, HD)
            prefill_step(request, head, keys, values, bias)

    def decode_group(group, place):
        row = lax.broadcasted_iota(jnp.int32, (8, HD), 0)
        parts = []
        for i in range(GROUP):
            scores = lax.dot_general(
                spread[plan[2, group * GROUP + i]],
                key_buf[place, i],
                (((1,), (1,)), ((), ())),
                preferred_element_type=jnp.float32,
            )
            valid = lanes < plan[1, group * GROUP + i]
            scores = jnp.where(valid, scores, NEG)
            top = jnp.max(scores, axis=1, keepdims=True)
            weights = jnp.where(valid, jnp.exp((scores - top) * SCALE), 0.0)
            total = jnp.sum(weights, axis=1, keepdims=True)
            product = jnp.dot(
                weights.astype(jnp.bfloat16),
                value_buf[place, i],
                preferred_element_type=jnp.float32,
            )
            value = jnp.zeros((8, HD), jnp.float32)
            for head in range(heads):
                value = jnp.where(row == head, product[:8, head * HD : (head + 1) * HD], value)
            parts.append((top[:8], total[:8], value))
        for i in range(GROUP):
            token = plan[2, group * GROUP + i]
            top, total, value = parts[i]
            before = dec_m[token]
            now = jnp.maximum(before, top)
            fade = jnp.exp((before - now) * SCALE)
            fresh = jnp.exp((top - now) * SCALE)
            dec_m[token] = now
            dec_l[token] = dec_l[token] * fade + total * fresh
            dec_o[token] = dec_o[token] * fade + value * fresh

    @pl.loop(0, end_all)
    def _(group):
        fetch(group + (BUFFERS - 1))
        for copy in copies(group):
            copy.wait()
        place = lax.rem(group, BUFFERS)

        @pl.when(group < end_prefill)
        def _():
            prefill_group(group, place)

        @pl.when(group >= end_prefill)
        def _():
            decode_group(group, place)

    width = heads * HD
    lane = lax.broadcasted_iota(jnp.int32, (SPAN, PAGE), 1)
    for request in range(PRE):
        rows = slice(request * SPAN, (request + 1) * SPAN)
        stats = jnp.zeros((SPAN, PAGE), jnp.float32)
        for head in range(heads):
            total = run_l[request, head]
            packed[rows, head * HD : (head + 1) * HD] = (
                run_o[request, head] / jnp.where(total > 0.0, total, 1.0)
            ).astype(jnp.bfloat16)
            pieces = split_bf16(run_m[request, head], 3) + split_bf16(total, 2)
            for j, piece in enumerate(pieces):
                stats = jnp.where(lane == head * 5 + j, piece, stats)
        packed[rows, width : width + PAGE] = stats.astype(jnp.bfloat16)
    total = dec_l[...]
    decode_out[...] = dec_o[...] / jnp.where(total > 0.0, total, 1.0)
    lane = lax.broadcasted_iota(jnp.int32, (DEC, 8, HD), 2)
    stats = jnp.zeros((DEC, 8, HD), jnp.float32)
    for j, piece in enumerate(split_bf16(dec_m[...], 3) + split_bf16(total, 2)):
        stats = jnp.where(lane == j, piece, stats)
    decode_stats[...] = stats


def attention(plan, queries, new_keys, new_values, key_cache, value_cache, first):
    width = queries.shape[1]
    heads = width // HD
    dec_q = queries[PRE * SPAN :]
    head_of = jnp.arange(width, dtype=jnp.int32) // HD
    own = head_of[None, :] == jnp.arange(ROWS, dtype=jnp.int32)[:, None]
    spread = jnp.where(own[None], dec_q[:, None, :], jnp.zeros((), dec_q.dtype))

    def by_head(rows):
        split = rows.astype(jnp.float32).reshape(DEC, heads, HD)
        return jnp.pad(split, ((0, 0), (0, 8 - heads), (0, 0)))

    self_score = jnp.sum(
        by_head(dec_q) * by_head(new_keys[PRE * SPAN :]), axis=2, keepdims=True
    )
    start_m = jnp.broadcast_to(jnp.where(first, self_score, NEG), (DEC, 8, HD))
    start_l = jnp.broadcast_to(jnp.where(first, 1.0, 0.0), (DEC, 8, HD)).astype(jnp.float32)
    start_o = jnp.where(first, by_head(new_values[PRE * SPAN :]), 0.0)
    vmem = pl.BlockSpec(memory_space=pltpu.VMEM)
    packed, decode_out, decode_stats = pl.pallas_call(
        functools.partial(attention_kernel, heads),
        out_shape=(
            jax.ShapeDtypeStruct((PRE * SPAN, width + PAGE), jnp.bfloat16),
            jax.ShapeDtypeStruct((DEC, 8, HD), jnp.float32),
            jax.ShapeDtypeStruct((DEC, 8, HD), jnp.float32),
        ),
        in_specs=[pl.BlockSpec(memory_space=pltpu.SMEM)]
        + [vmem] * 7
        + [pl.BlockSpec(memory_space=pl.ANY)] * 2,
        out_specs=(vmem, vmem, vmem),
        scratch_shapes=[
            pltpu.VMEM((BUFFERS, GROUP, PAGE, width), jnp.bfloat16),
            pltpu.VMEM((BUFFERS, GROUP, PAGE, width), jnp.bfloat16),
            pltpu.VMEM((PRE, heads, SPAN, HD), jnp.float32),
            pltpu.VMEM((PRE, heads, SPAN, HD), jnp.float32),
            pltpu.VMEM((PRE, heads, SPAN, HD), jnp.float32),
            pltpu.VMEM((DEC, 8, HD), jnp.float32),
            pltpu.VMEM((DEC, 8, HD), jnp.float32),
            pltpu.VMEM((DEC, 8, HD), jnp.float32),
            pltpu.SemaphoreType.DMA((BUFFERS, 2, GROUP)),
        ],
        compiler_params=pltpu.CompilerParams(vmem_limit_bytes=40 * 1024 * 1024),
        name="paged_attention",
    )(plan, queries, new_keys, new_values, spread, start_m, start_l, start_o, key_cache, value_cache)
    dec_rows = jnp.concatenate(
        [
            decode_out[:, :heads].reshape(DEC, width),
            jnp.pad(
                decode_stats[:, :heads, :5].reshape(DEC, heads * 5),
                ((0, 0), (0, PAGE - heads * 5)),
            ),
        ],
        axis=1,
    ).astype(jnp.bfloat16)
    return jnp.concatenate([packed, dec_rows], axis=0)


def page_plan(page_table, span_offsets, decode_lengths, first_page, page_count, first):
    local_ids = first_page + jnp.arange(page_count, dtype=jnp.int32)
    flat = page_table.reshape(-1)
    code = jnp.max(
        jnp.where(
            flat[None, :] == local_ids[:, None],
            jnp.arange(1, flat.shape[0] + 1, dtype=jnp.int32)[None, :],
            0,
        ),
        axis=1,
    )
    owner = (code - 1) // MAXP
    slot = (code - 1) % MAXP
    prefixes = jnp.concatenate([span_offsets, decode_lengths])
    request = jnp.arange(PRE + DEC, dtype=jnp.int32)
    prefix = jnp.sum(jnp.where(owner[:, None] == request[None, :], prefixes[None, :], 0), axis=1)
    count = jnp.where(code > 0, jnp.clip(prefix - slot * PAGE, 0, PAGE), 0)
    kind = jnp.where(count > 0, jnp.minimum(owner, PRE), PRE + 1)
    sizes = jnp.sum(kind[None, :] == jnp.arange(PRE + 1, dtype=jnp.int32)[:, None], axis=1)
    groups = (sizes + GROUP - 1) // GROUP
    ends = jnp.stack([groups[0], groups[0] + groups[1], groups[0] + groups[1] + groups[2]])
    begin = jnp.where(kind == 0, 0, jnp.where(kind == 1, ends[0], ends[1])) * GROUP
    index = jnp.arange(page_count, dtype=jnp.int32)
    rank = jnp.sum((kind[None, :] == kind[:, None]) & (index[None, :] < index[:, None]), axis=1)
    place = jnp.where(kind <= PRE, begin + rank, -1)
    hit = place[None, :] == jnp.arange(SLOTS, dtype=jnp.int32)[:, None]
    token = jnp.maximum(owner - PRE, 0)

    def listed(values):
        return jnp.sum(jnp.where(hit, values[None, :], 0), axis=1).astype(jnp.int32)

    last = jnp.concatenate([ends, first.astype(jnp.int32)[None]]).astype(jnp.int32)
    return jnp.stack(
        [listed(index), listed(count), listed(token), jnp.pad(last, (0, SLOTS - 4))]
    )


def join_parts(parts, heads):
    devices, tokens = parts.shape[0], parts.shape[1]
    width = heads * HD
    parts = parts.astype(jnp.float32)
    outs = parts[:, :, :width].reshape(devices, tokens, heads, HD)
    stats = parts[:, :, width : width + heads * 5].reshape(devices, tokens, heads, 5)
    maxima = stats[..., 0] + stats[..., 1] + stats[..., 2]
    share = (stats[..., 3] + stats[..., 4]) * jnp.exp((maxima - jnp.max(maxima, axis=0)) * SCALE)
    joined = jnp.sum(outs * share[..., None], axis=0) / jnp.sum(share, axis=0)[..., None]
    return joined.astype(jnp.bfloat16).reshape(tokens, width)


def shards(
    layer_input,
    norm_gain,
    qkv_weight,
    key_cache,
    value_cache,
    out_weight,
    ffn_gain,
    gate_up_weight,
    down_weight,
    span_offsets,
    decode_lengths,
    page_table,
):
    group_width = qkv_weight.shape[2]
    group_heads = group_width // HD
    n_ffn, n_grp = lax.axis_size("ffn"), lax.axis_size("grp")
    first = lax.axis_index("ffn") == 0
    page_count = key_cache.shape[0]
    plan = page_plan(
        page_table,
        span_offsets,
        decode_lengths,
        lax.axis_index("ffn") * page_count,
        page_count,
        first,
    )
    input_f32 = layer_input.astype(jnp.float32)
    scaled = (input_f32 * norm_gain[None, :]).astype(jnp.bfloat16)
    squares = jnp.sum(input_f32 * input_f32, axis=1)
    positions = token_positions(span_offsets, decode_lengths)
    partial_value = jnp.concatenate(
        [
            jnp.dot(scaled, qkv_weight[k], preferred_element_type=jnp.float32).astype(jnp.bfloat16)
            for k in range(3)
        ]
        + [jnp.broadcast_to(squares[:, None], (TOKENS, HD)).astype(jnp.bfloat16)],
        axis=1,
    )
    reduced = lax.psum(partial_value, "ffn").astype(jnp.float32)
    summed = reduced[:, : 3 * group_width].reshape(TOKENS, 3, group_width)
    fresh = finish_projection(summed, reduced[:, 3 * group_width], positions, group_heads)
    packed = attention(
        plan, fresh[:, 0], fresh[:, 1], fresh[:, 2], key_cache, value_cache, first
    )
    parts = lax.all_to_all(
        packed.reshape(n_ffn, TOKENS // n_ffn, packed.shape[1]), "ffn", 0, 0
    )
    heads_out = lax.all_gather(join_parts(parts, group_heads), "ffn", axis=0, tiled=True)
    head_part = jnp.dot(heads_out, out_weight, preferred_element_type=jnp.float32)
    quarter = TOKENS // n_grp
    blocks = lax.all_to_all(
        head_part.astype(jnp.bfloat16).reshape(n_grp, quarter, head_part.shape[1]), "grp", 0, 0
    )
    own_input = lax.dynamic_slice_in_dim(layer_input, lax.axis_index("grp") * quarter, quarter, 0)
    own_block = (
        own_input.astype(jnp.float32) + jnp.sum(blocks.astype(jnp.float32), axis=0)
    ).astype(jnp.bfloat16)
    block_rows = lax.all_gather(own_block, "ffn", axis=1, tiled=True)
    rows_f32 = block_rows.astype(jnp.float32)
    inverse = lax.rsqrt(jnp.sum(rows_f32 * rows_f32, axis=1) / D + EPS)[:, None]
    normed = (rows_f32 * inverse * ffn_gain[None, :]).astype(jnp.bfloat16)
    gate_up = jnp.einsum("td,kdf->ktf", normed, gate_up_weight, preferred_element_type=jnp.float32)
    hidden = (jax.nn.silu(gate_up[0]) * gate_up[1]).astype(jnp.bfloat16)
    down_terms = jnp.dot(hidden, down_weight, preferred_element_type=jnp.float32)
    pieces = lax.all_to_all(
        down_terms.astype(jnp.bfloat16).reshape(quarter, n_ffn, D // n_ffn).swapaxes(0, 1),
        "ffn",
        0,
        0,
    )
    summed_out = jnp.sum(pieces.astype(jnp.float32), axis=0)
    return (own_block.astype(jnp.float32) + summed_out).astype(jnp.bfloat16)


def solution(mesh):
    in_specs = (
        P(None, "ffn"),
        P("ffn"),
        P(None, "ffn", "grp"),
        P("ffn", None, "grp"),
        P("ffn", None, "grp"),
        P("grp", "ffn"),
        P(),
        P(None, None, "ffn"),
        P("ffn", None),
        P(),
        P(),
        P(),
    )
    out_specs = P("grp", "ffn")
    return jax.shard_map(shards, mesh=mesh, in_specs=in_specs, out_specs=out_specs, check_vma=False)
```

time: 692 us -> 250 us (0.36); the launches traced: 685 us -> 250 us
  local copies, waits for them, and re-layouts: 275 us -> 20.6 us
  matrix products: 159 us -> 31.9 us
  other arithmetic: 97.3 us -> 10.2 us
  Pallas kernels: 0 us -> 35.5 us
  waiting for transfers between devices: 76.7 us -> 63.1 us
    gather x7 -> x0, local copies, waits for them, and re-layouts: 172 us -> none  [the longest x2 64.7 us: shards(): new_keys[key_rows]]
    dot_general x7 -> x3, matrix products: 132 us -> 5.28 us  [shards(): jnp.dot(scaled, qkv_weight[k], preferred_element_type=jnp.float32)]
    unnamed x34 -> x30, local copies, waits for them, and re-layouts: 50.8 us -> 1.24 us
    all_to_all x0 -> x2, blocking collectives: none -> 39.4 us  [the longest x1 22.3 us: shards(): lax.all_to_all(down_terms.astype(jnp.bfloat16).reshape(quarter, n_ffn, D...]
    reshape x1 -> x4, local copies, waits for them, and re-layouts: 39.4 us -> 2.81 us  [the longest x1 2.56 us: shards(): summed = reduced[:, :3 * group_width].reshape(TOKENS, 3, group_width)]
    select_n x4 -> x7, other arithmetic: 36.4 us -> 0.78 us  [the longest x1 0.63 us: page_plan(): place = jnp.where(kind <= PRE, begin + rank, -1)]
    pallas_call x0 -> x1, Pallas kernels: none -> 35.5 us  [attention(): pl.pallas_call(functools.partial(attention_kernel, heads), out_shape=(jax...]
    unnamed x5 -> x1, waiting for transfers between devices: 33.9 us -> 0.02 us
  transfers between devices with their start and end apart: 4 -> 2, of which waited for: 2 -> 2; matrix products, arithmetic and copies ran while one was open for 11% -> 2% of each run, Pallas kernels for 0% -> 0%
where the time goes in v1:
time: 250 us
  blocking collectives  69.6 us (28%)
  waiting for transfers between devices  63.1 us (25%)
  Pallas kernels  35.5 us (14%)
  matrix products  31.9 us (13%)
  local copies, waits for them, and re-layouts  20.6 us (8%)
  between operations  15.8 us (6%)
  other arithmetic  10.2 us (4%)
  starting transfers between devices  3.63 us (1%)
    psum x1, waiting for transfers between devices, shards(): reduced = lax.psum(partial_value, 'ffn').astype(jnp.float32)  56.1 us
    pallas_call x1, Pallas kernels, attention(): pl.pallas_call(functools.partial(attention_kernel, heads), out_shape=(jax...  35.5 us
    all_to_all x1, blocking collectives, shards(): lax.all_to_all(down_terms.astype(jnp.bfloat16).reshape(quarter, n_ffn, D...  22.3 us
    all_to_all x1, blocking collectives, shards(): lax.all_to_all(packed.reshape(n_ffn, TOKENS // n_ffn, packed.shape[1]), '...  17.1 us
    dot_general x1, matrix products, shards(): jnp.einsum('td,kdf->ktf', normed, gate_up_weight, preferred_element_type=...  16.1 us
    all_gather x1, blocking collectives, shards(): block_rows = lax.all_gather(own_block, 'ffn', axis=1, tiled=True)  15.6 us
    all_gather x1, blocking collectives, shards(): lax.all_gather(join_parts(parts, group_heads), 'ffn', axis=0, tiled=True)  14.6 us
    dot_general x1, matrix products, shards(): jnp.dot(hidden, down_weight, preferred_element_type=jnp.float32)  9.31 us
  transfers between devices with their start and end apart: 2, of which 2 were waited for; matrix products, arithmetic and copies ran while one was open for 2% of the time, Pallas kernels for 0%

profile of v1, /device:TPU:0, one launch (start us, length us, event | category | flops | bytes accessed | tf_op | source)
XLA Modules:
  0.0 250.4 jit_solution(5921824498564642002)
XLA Ops:
  6.5 1.9 convolution_convert_fusion.2
  8.4 1.8 convolution_convert_fusion.3
  10.2 1.6 convolution_convert_fusion.4
  11.9 0.2 fusion.14
  12.1 0.1 broadcast_in_dim.165
  12.2 1.2 pad_maximum_fusion
  13.4 0.1 add_bitcast_fusion
  13.5 0.4 select_reduce_fusion
  13.9 0.1 pad_add_fusion.1
  14.0 0.1 select_reduce_fusion.4
  14.1 0.1 convert_reduce_fusion.3
  14.2 0.2 convert_reduce_fusion.2
  14.5 0.6 fusion.50
  17.0 0.7 pad_add_fusion.2
  17.7 0.6 compare_select_fusion.2
  18.3 0.1 select_reduce_fusion.3
  18.5 1.1 multiply_cosine_fusion
  19.6 56.1 %all-reduce.7.cloned.1.call-done = bf16[288,2048]{1,0:T(8,128)(2,1)} async-done(((bf16[288,2048]{1,0:T(8,128)(2,1)}), bf16[288,2048]{1,0:T(8,128)(2,1)}) %all-reduce.7.cloned.1.call-update) | async-done | bytes 1179664 | tf_op jit(solution)/shard_map/psum | solution.py:404
  75.8 1.4 slice.138
  77.2 2.6 %reshape.321 = f32[288,3,640]{2,1,0:T(4,128)} reshape(f32[288,1920]{1,0:T(8,128)S(1)} %slice.138) | data formatting | bytes 4423680 | tf_op jit(solution)/shard_map/reshape | solution.py:405
  79.7 6.7 %fusion.49 = (f32[288,1,640]{2,1,0:T(1,128)S(1)}, f32[288,1,640]{2,1,0:T(1,128)S(1)}, f32[288,1,640]{2,1,0:T(1,128)}) fusion(f32[288,3,640]{2,1,0:T(4,128)} %reshape.321), kind=kLoop, calls=%fused_computation.137 | loop fusion | bytes 4423680 | tf_op jit(solution)/shard_map/slice | solution.py:57
  86.4 3.2 %copy.41 = f32[288,1,640]{0,2,1:T(8,128)} copy(f32[288,1,640]{2,1,0:T(1,128)} %get-tuple-element.22) | data formatting | bytes 1474560 | tf_op jit(solution)/shard_map/slice | solution.py:55
  89.5 2.0 copy.42
  91.6 0.3 convert_element_type.106
  91.8 0.1 fusion.33
  92.0 0.8 copy-done.3
  92.8 0.3 copy-done.4
  93.1 0.1 broadcast_multiply_fusion
  93.2 0.3 subtract_convert_fusion
  93.5 0.1 fusion.29
  93.6 0.9 pad_maximum_fusion.1
  94.5 0.9 fusion.17
  95.3 0.1 fusion.55.new_values
  95.4 0.1 multiply_reduce_fusion
  95.5 0.1 copy.45
  95.6 0.1 copy.55
  95.7 1.2 copy.46.queries
  97.0 0.2 copy.47.new_keys
  97.3 0.1 broadcast_select_fusion.spread
  97.4 0.1 broadcast_in_dim.171.start_m
  97.6 35.5 %paged_attention.1 = (bf16[256,768]{1,0:T(8,128)(2,1)S(1)}, f32[32,8,128]{2,1,0:T(8,128)S(1)}, f32[32,8,128]{2,1,0:T(8,128)S(1)}) custom-call(s32[4,128]{1,0:T(4,128)S(1)} %pad_add_fusion.plan, bf16[288,640]{1,0:T(8,128)(2,1)S(1)} %copy.46.queries, bf16[288,640]{1,0:T(8,128)(2,1)S(1)} %copy.47.new_keys, bf16[288,640]{1,0:T(8,128)(2,1)S(1)} %fusion.55.new_values, ...), custom_call_target="tpu_custom_call" | custom-call | tf_op jit(solution)/shard_map/paged_attention/pallas_call | solution.py:278
  133.2 0.1 reshape.332
  133.3 0.1 reshape.324
  133.4 17.1 %all_to_all.15 = bf16[8,36,768]{2,1,0:T(8,128)(2,1)S(1)} all-to-all(bf16[8,36,768]{2,1,0:T(8,128)(2,1)S(1)} %reshape.324), channel_id=1, replica_groups=mesh['grp'=4,'ffn'=8] {'ffn'}, dimensions={0} | all-to-all | bytes 884736 | tf_op jit(solution)/shard_map/all_to_all | solution.py:410
  150.5 0.1 copy.50
  150.7 0.1 copy.53
  150.8 0.1 div.71
  150.9 0.1 copy.51
  151.1 0.3 broadcast_bitcast_fusion
  151.3 0.1 convert_element_type.109
  151.4 0.2 fusion.6
  151.6 14.6 %all-gather = bf16[8,36,640]{2,1,0:T(8,128)(2,1)S(1)} all-gather(bf16[1,36,640]{2,1,0:T(8,128)(2,1)S(1)} %fusion.35), channel_id=1, replica_groups=mesh['grp'=4,'ffn'=8] {'ffn'}, dimensions={0}, use_global_device_ids=true | all-gather | bytes 414720 | tf_op jit(solution)/shard_map/all_gather | solution.py:413
  166.2 0.1 reshape.330
  166.3 1.2 convolution_convert_fusion.1
  167.5 3.6 %all-to-all-start.1 = ((bf16[4,72,640]{2,1,0:T(8,128)(2,1)}), bf16[4,72,640]{2,1,0:T(8,128)(2,1)S(1)}, u32[]{:S(2)}, u32[]{:S(2)}) async-start(bf16[4,72,640]{2,1,0:T(8,128)(2,1)} %bitcast.27), calls=%async_computation.1 | async-start | bytes 737280 | tf_op jit(solution)/shard_map/all_to_all | solution.py:416
  171.2 6.9 %all-to-all-done.1 = bf16[4,72,640]{2,1,0:T(8,128)(2,1)S(1)} async-done(((bf16[4,72,640]{2,1,0:T(8,128)(2,1)}), bf16[4,72,640]{2,1,0:T(8,128)(2,1)S(1)}, u32[]{:S(2)}, u32[]{:S(2)}) %all-to-all-start.1) | async-done | bytes 368672 | tf_op jit(solution)/shard_map/all_to_all | solution.py:416
  178.1 0.9 add_convert_fusion.3
  179.1 15.6 %all_gather.7 = bf16[72,5120]{1,0:T(8,128)(2,1)S(1)} all-gather(bf16[72,640]{1,0:T(8,128)(2,1)S(1)} %add_convert_fusion.3), channel_id=1, replica_groups=mesh['grp'=4,'ffn'=8] {'ffn'}, dimensions={1}, use_global_device_ids=true | all-gather | bytes 829440 | tf_op jit(solution)/shard_map/all_gather | solution.py:423
  194.7 0.3 fusion
  195.0 16.1 %convolution_bitcast_fusion = f32[2,72,1728]{2,1,0:T(8,128)S(1)} fusion(bf16[2,5120,1728]{1,2,0:T(8,128)(2,1)} %param.19, bf16[72,5120]{1,0:T(8,128)(2,1)S(1)} %all_gather.7, f32[5120]{0:T(1024)S(1)} %copy-done.8, f32[72]{0:T(128)S(1)} %add_rsqrt_fusion), kind=kOutput, calls=%fused_computation.1 | convolution fusion | flops 2549514240 | bytes 37142816 | tf_op jit(solution)/shard_map/td,kdf->ktf/dot_general | solution.py:427
  211.0 9.3 %convolution_convert_fusion = bf16[72,5120]{1,0:T(8,128)(2,1)S(1)} fusion(bf16[1728,5120]{1,0:T(8,128)(2,1)} %param.20, f32[2,72,1728]{2,1,0:T(8,128)S(1)} %convolution_bitcast_fusion), kind=kOutput, calls=%fused_computation | convolution fusion | flops 1275134976 | bytes 19427328 | tf_op jit(solution)/shard_map/dot_general | solution.py:429
  220.4 22.3 %all_to_all.16 = bf16[8,72,640]{2,1,0:T(8,128)(2,1)S(1)} all-to-all(bf16[8,72,640]{2,1,0:T(8,128)(2,1)S(1)} %bitcast.90), channel_id=1, replica_groups=mesh['grp'=4,'ffn'=8] {'ffn'}, dimensions={0} | all-to-all | bytes 1474560 | tf_op jit(solution)/shard_map/all_to_all | solution.py:430
  242.8 0.1 convert_reduce_fusion
  242.9 0.7 add_convert_fusion.2
  (57 shorter events, 0.6 us)
Async XLA Ops:
  6.5 159.7 %copy-start = (bf16[640,640]{1,0:T(8,128)(2,1)S(1)}, bf16[640,640]{1,0:T(8,128)(2,1)}, u32[]{:S(2)}) copy-start(bf16[640,640]{1,0:T(8,128)(2,1)} %param.17) | copy-start | bytes 2457604
  6.5 3.7 %copy-start.5 = (bf16[288,640]{1,0:T(8,128)(2,1)S(1)}, bf16[288,640]{1,0:T(8,128)(2,1)}, u32[]{:S(2)}) copy-start(bf16[288,640]{1,0:T(8,128)(2,1)} %param.12) | copy-start | bytes 1105924
  6.5 3.7 %copy-start.11 = (f32[640]{0:T(1024)S(1)}, f32[640]{0:T(1024)}, u32[]{:S(2)}) copy-start(f32[640]{0:T(1024)} %param.13) | copy-start | bytes 7684
  6.5 69.2 %all-reduce.7.cloned.1.call-start = ((), (), s32[]{:S(2)}) async-start(), calls=%async_computation.3 | async-start | bytes 2359296 | tf_op jit(solution)/shard_map/psum | solution.py:404
  11.9 1.5 copy-start.12
  11.9 1.6 copy-start.9
  11.9 2.0 copy-start.10
  86.4 5.2 %copy-start.2 = (bf16[288,2048]{1,0:T(8,128)(2,1)S(1)}, bf16[288,2048]{1,0:T(8,128)(2,1)}, u32[]{:S(2)}) copy-start(bf16[288,2048]{1,0:T(8,128)(2,1)} %all-reduce.7.cloned.1.call-done) | copy-start | bytes 3538948
  91.6 1.2 copy-start.3
  91.6 1.5 copy-start.4
  91.8 1.4 copy-start.6
  91.8 1.4 copy-start.7
  95.3 1.9 slice-start
  166.3 28.7 %copy-start.8 = (f32[5120]{0:T(1024)S(1)}, f32[5120]{0:T(1024)}, u32[]{:S(2)}) copy-start(f32[5120]{0:T(1024)} %param.18) | copy-start | bytes 61444
  167.5 10.6 %all-to-all-start.1 = ((bf16[4,72,640]{2,1,0:T(8,128)(2,1)}), bf16[4,72,640]{2,1,0:T(8,128)(2,1)S(1)}, u32[]{:S(2)}, u32[]{:S(2)}) async-start(bf16[4,72,640]{2,1,0:T(8,128)(2,1)} %bitcast.27), calls=%async_computation.1 | async-start | bytes 737280 | tf_op jit(solution)/shard_map/all_to_all | solution.py:416
  211.0 32.5 %copy-start.1 = (bf16[640,640]{1,0:T(8,128)(2,1)S(1)}, bf16[640,640]{1,0:T(8,128)(2,1)}, u32[]{:S(2)}) copy-start(bf16[640,640]{1,0:T(8,128)(2,1)} %param.17) | copy-start | bytes 2457604
Sparse Core Ops, SparseCore 0:
  13.5 62.2 all-reduce.6

commit v2 on v1

--- a/solution.py
+++ b/solution.py
@@ -27,19 +27,15 @@
 ROWS = 16
 
 
-def rotate(values, positions):
-    half_width = values.shape[-1] // 2
+def rotary_tables(positions):
     frequency = jnp.exp(
-        jnp.arange(half_width, dtype=jnp.float32) * (-2.0 * math.log(10000.0) / values.shape[-1])
+        jnp.arange(HD // 2, dtype=jnp.float32) * (-2.0 * math.log(10000.0) / HD)
     )
     angles = positions.astype(jnp.float32)[:, None] * frequency[None, :]
-    cosine = jnp.cos(angles)[:, None, :]
-    sine_table = jnp.sin(angles)[:, None, :]
-    leading = values[..., :half_width]
-    trailing = values[..., half_width:]
-    return jnp.concatenate(
-        [leading * cosine - trailing * sine_table, trailing * cosine + leading * sine_table],
-        axis=-1,
+    cosine, sine = jnp.cos(angles), jnp.sin(angles)
+    return (
+        jnp.concatenate([cosine, cosine], axis=1),
+        jnp.concatenate([-sine, sine], axis=1),
     )
 
 
@@ -49,14 +45,19 @@
     return jnp.concatenate([prefill, decode_lengths])
 
 
-def finish_projection(summed, squares, positions, group_heads):
-    inverse = lax.rsqrt(squares / D + EPS)[:, None]
-    row_count = summed.shape[0]
-    queries = rotate((summed[:, 0] * inverse).reshape(row_count, group_heads, HD), positions)
-    fresh_keys = rotate((summed[:, 1] * inverse).reshape(row_count, group_heads, HD), positions)
-    fresh_values = (summed[:, 2] * inverse).reshape(row_count, group_heads, HD)
-    stacked = jnp.stack([queries, fresh_keys, fresh_values], axis=1).astype(jnp.bfloat16)
-    return stacked.reshape(row_count, 3, group_heads * HD)
+def pair_groups(n):
+    return (
+        [[2 * chip, 2 * chip + 1] for chip in range(n // 2)],
+        [[2 * chip + core for chip in range(n // 2)] for core in range(2)],
+    )
+
+
+def scatter_sum(blocks):
+    pairs, chips = pair_groups(lax.axis_size("ffn"))
+    halves = lax.all_to_all(blocks, "ffn", 0, 0, axis_index_groups=pairs)
+    half = jnp.sum(halves.astype(jnp.float32), axis=0).astype(blocks.dtype)
+    parts = lax.all_to_all(half, "ffn", 0, 0, axis_index_groups=chips)
+    return jnp.sum(parts.astype(jnp.float32), axis=0)
 
 
 def split_bf16(value, pieces):
@@ -71,18 +72,18 @@
 def attention_kernel(
     heads,
     plan,
-    queries,
-    new_keys,
-    new_values,
-    spread,
-    start_m,
-    start_l,
-    start_o,
+    reduced,
+    cosine,
+    sine,
     key_cache,
     value_cache,
     packed,
     decode_out,
     decode_stats,
+    queries,
+    new_keys,
+    new_values,
+    spread,
     key_buf,
     value_buf,
     run_m,
@@ -124,9 +125,44 @@
     run_m[...] = jnp.full_like(run_m, NEG)
     run_l[...] = jnp.zeros_like(run_l)
     run_o[...] = jnp.zeros_like(run_o)
-    dec_m[...] = start_m[...]
-    dec_l[...] = start_l[...]
-    dec_o[...] = start_o[...]
+
+    width = heads * HD
+    squares = reduced[:, 3 * width : 3 * width + HD].astype(jnp.float32)
+    inverse = lax.rsqrt(squares / D + EPS)
+
+    def projected(which, head):
+        start = which * width + head * HD
+        return reduced[:, start : start + HD].astype(jnp.float32) * inverse
+
+    def turned(value):
+        swapped = jnp.concatenate([value[:, HD // 2 :], value[:, : HD // 2]], axis=1)
+        return value * cosine[...] + swapped * sine[...]
+
+    is_first = plan[3, 3] == 1
+    dec_row = lax.broadcasted_iota(jnp.int32, (DEC, 8, HD), 1)
+    spread_row = lax.broadcasted_iota(jnp.int32, (DEC, ROWS, HD), 1)
+    start_m = jnp.zeros((DEC, 8, HD), jnp.float32)
+    start_o = jnp.zeros((DEC, 8, HD), jnp.float32)
+    for head in range(heads):
+        columns = slice(head * HD, (head + 1) * HD)
+        query = turned(projected(0, head)).astype(jnp.bfloat16)
+        key = turned(projected(1, head)).astype(jnp.bfloat16)
+        value = projected(2, head).astype(jnp.bfloat16)
+        queries[:, columns] = query
+        new_keys[:, columns] = key
+        new_values[:, columns] = value
+        dec_q = query[PRE * SPAN :].astype(jnp.float32)
+        dec_k = key[PRE * SPAN :].astype(jnp.float32)
+        dec_v = value[PRE * SPAN :].astype(jnp.float32)
+        spread[:, :, columns] = jnp.where(spread_row == head, dec_q[:, None, :], 0.0).astype(
+            jnp.bfloat16
+        )
+        own = jnp.broadcast_to(jnp.sum(dec_q * dec_k, axis=1, keepdims=True), (DEC, HD))
+        start_m = jnp.where(dec_row == head, own[:, None, :], start_m)
+        start_o = jnp.where(dec_row == head, dec_v[:, None, :], start_o)
+    dec_m[...] = jnp.where(is_first, start_m, NEG)
+    dec_l[...] = jnp.full((DEC, 8, HD), jnp.where(is_first, 1.0, 0.0), jnp.float32)
+    dec_o[...] = jnp.where(is_first, start_o, 0.0)
 
     def prefill_step(request, head, keys, values, bias):
         columns = slice(head * HD, (head + 1) * HD)
@@ -233,7 +269,6 @@
         def _():
             decode_group(group, place)
 
-    width = heads * HD
     lane = lax.broadcasted_iota(jnp.int32, (SPAN, PAGE), 1)
     for request in range(PRE):
         rows = slice(request * SPAN, (request + 1) * SPAN)
@@ -256,24 +291,10 @@
     decode_stats[...] = stats
 
 
-def attention(plan, queries, new_keys, new_values, key_cache, value_cache, first):
-    width = queries.shape[1]
+def attention(plan, reduced, positions, key_cache, value_cache):
+    width = key_cache.shape[2]
     heads = width // HD
-    dec_q = queries[PRE * SPAN :]
-    head_of = jnp.arange(width, dtype=jnp.int32) // HD
-    own = head_of[None, :] == jnp.arange(ROWS, dtype=jnp.int32)[:, None]
-    spread = jnp.where(own[None], dec_q[:, None, :], jnp.zeros((), dec_q.dtype))
-
-    def by_head(rows):
-        split = rows.astype(jnp.float32).reshape(DEC, heads, HD)
-        return jnp.pad(split, ((0, 0), (0, 8 - heads), (0, 0)))
-
-    self_score = jnp.sum(
-        by_head(dec_q) * by_head(new_keys[PRE * SPAN :]), axis=2, keepdims=True
-    )
-    start_m = jnp.broadcast_to(jnp.where(first, self_score, NEG), (DEC, 8, HD))
-    start_l = jnp.broadcast_to(jnp.where(first, 1.0, 0.0), (DEC, 8, HD)).astype(jnp.float32)
-    start_o = jnp.where(first, by_head(new_values[PRE * SPAN :]), 0.0)
+    cosine, sine = rotary_tables(positions)
     vmem = pl.BlockSpec(memory_space=pltpu.VMEM)
     packed, decode_out, decode_stats = pl.pallas_call(
         functools.partial(attention_kernel, heads),
@@ -283,10 +304,14 @@
             jax.ShapeDtypeStruct((DEC, 8, HD), jnp.float32),
         ),
         in_specs=[pl.BlockSpec(memory_space=pltpu.SMEM)]
-        + [vmem] * 7
+        + [vmem] * 3
         + [pl.BlockSpec(memory_space=pl.ANY)] * 2,
         out_specs=(vmem, vmem, vmem),
         scratch_shapes=[
+            pltpu.VMEM((TOKENS, width), jnp.bfloat16),
+            pltpu.VMEM((TOKENS, width), jnp.bfloat16),
+            pltpu.VMEM((TOKENS, width), jnp.bfloat16),
+            pltpu.VMEM((DEC, ROWS, width), jnp.bfloat16),
             pltpu.VMEM((BUFFERS, GROUP, PAGE, width), jnp.bfloat16),
             pltpu.VMEM((BUFFERS, GROUP, PAGE, width), jnp.bfloat16),
             pltpu.VMEM((PRE, heads, SPAN, HD), jnp.float32),
@@ -299,7 +324,7 @@
         ],
         compiler_params=pltpu.CompilerParams(vmem_limit_bytes=40 * 1024 * 1024),
         name="paged_attention",
-    )(plan, queries, new_keys, new_values, spread, start_m, start_l, start_o, key_cache, value_cache)
+    )(plan, reduced, cosine, sine, key_cache, value_cache)
     dec_rows = jnp.concatenate(
         [
             decode_out[:, :heads].reshape(DEC, width),
@@ -401,12 +426,15 @@
         + [jnp.broadcast_to(squares[:, None], (TOKENS, HD)).astype(jnp.bfloat16)],
         axis=1,
     )
-    reduced = lax.psum(partial_value, "ffn").astype(jnp.float32)
-    summed = reduced[:, : 3 * group_width].reshape(TOKENS, 3, group_width)
-    fresh = finish_projection(summed, reduced[:, 3 * group_width], positions, group_heads)
-    packed = attention(
-        plan, fresh[:, 0], fresh[:, 1], fresh[:, 2], key_cache, value_cache, first
-    )
+    pairs, chips = pair_groups(n_ffn)
+    columns = partial_value.shape[1] // n_ffn
+    own_sum = scatter_sum(
+        partial_value.reshape(TOKENS, 2, n_ffn // 2, columns).transpose(1, 2, 0, 3)
+    ).astype(jnp.bfloat16)
+    of_core = lax.all_gather(own_sum, "ffn", axis_index_groups=chips)
+    gathered = lax.all_gather(of_core, "ffn", axis_index_groups=pairs)
+    reduced = gathered.transpose(2, 0, 1, 3).reshape(partial_value.shape)
+    packed = attention(plan, reduced, positions, key_cache, value_cache)
     parts = lax.all_to_all(
         packed.reshape(n_ffn, TOKENS // n_ffn, packed.shape[1]), "ffn", 0, 0
     )
@@ -427,13 +455,11 @@
     gate_up = jnp.einsum("td,kdf->ktf", normed, gate_up_weight, preferred_element_type=jnp.float32)
     hidden = (jax.nn.silu(gate_up[0]) * gate_up[1]).astype(jnp.bfloat16)
     down_terms = jnp.dot(hidden, down_weight, preferred_element_type=jnp.float32)
-    pieces = lax.all_to_all(
-        down_terms.astype(jnp.bfloat16).reshape(quarter, n_ffn, D // n_ffn).swapaxes(0, 1),
-        "ffn",
-        0,
-        0,
-    )
-    summed_out = jnp.sum(pieces.astype(jnp.float32), axis=0)
+    summed_out = scatter_sum(
+        down_terms.astype(jnp.bfloat16)
+        .reshape(quarter, n_ffn // 2, 2, D // n_ffn)
+        .transpose(2, 1, 0, 3)
+    )
     return (own_block.astype(jnp.float32) + summed_out).astype(jnp.bfloat16)
 
 

time: 250 us -> 229 us (0.916)
  waiting for transfers between devices: 63.1 us -> 25.2 us
  blocking collectives: 69.6 us -> 90.5 us
  local copies, waits for them, and re-layouts: 20.6 us -> 10.8 us
  starting transfers between devices: 3.63 us -> 10.1 us
    psum x1 -> x0, waiting for transfers between devices: 56.1 us -> none  [shards(): reduced = lax.psum(partial_value, 'ffn').astype(jnp.float32)]
    all_gather x0 -> x1, blocking collectives: none -> 17.2 us  [shards(): of_core = lax.all_gather(own_sum, 'ffn', axis_index_groups=chips)]
    slice x6 -> x0, local copies, waits for them, and re-layouts: 13.2 us -> none  [the longest x1 6.66 us: finish_projection(): fresh_values = (summed[:, 2] * inverse).reshape(row_count, group_heads, HD)]
    all_to_all x0 -> x1, waiting for transfers between devices: none -> 12.8 us  [scatter_sum(): parts = lax.all_to_all(half, 'ffn', 0, 0, axis_index_groups=chips)]
    all_to_all x0 -> x1, starting transfers between devices: none -> 6.31 us  [scatter_sum(): parts = lax.all_to_all(half, 'ffn', 0, 0, axis_index_groups=chips)]
    all_gather x0 -> x1, waiting for transfers between devices: none -> 5.5 us  [shards(): gathered = lax.all_gather(of_core, 'ffn', axis_index_groups=pairs)]
    all_gather x0 -> x1, local copies, waits for them, and re-layouts: none -> 3.23 us  [shards(): gathered = lax.all_gather(of_core, 'ffn', axis_index_groups=pairs)]
    all_to_all x1, blocking collectives: 17.1 us -> 19.9 us  [shards(): lax.all_to_all(packed.reshape(n_ffn, TOKENS // n_ffn, packed.shape[1]), '...]
  transfers between devices with their start and end apart: 2 -> 3, of which waited for: 2 -> 3; matrix products, arithmetic and copies ran while one was open for 2% -> 2% of each run, Pallas kernels for 0% -> 0%
where the time goes in v2:
time: 229 us
  blocking collectives  90.5 us (40%)
  Pallas kernels  37.1 us (16%)
  matrix products  31.6 us (14%)
  waiting for transfers between devices  25.2 us (11%)
  between operations  15.6 us (7%)
  local copies, waits for them, and re-layouts  10.8 us (5%)
  starting transfers between devices  10.1 us (4%)
  other arithmetic  8.12 us (4%)
    pallas_call x1, Pallas kernels, attention(): pl.pallas_call(functools.partial(attention_kernel, heads), out_shape=(jax...  37.1 us
    all_to_all x1, blocking collectives, shards(): lax.all_to_all(packed.reshape(n_ffn, TOKENS // n_ffn, packed.shape[1]), '...  19.9 us
    all_gather x1, blocking collectives, shards(): of_core = lax.all_gather(own_sum, 'ffn', axis_index_groups=chips)  17.2 us
    dot_general x1, matrix products, shards(): jnp.einsum('td,kdf->ktf', normed, gate_up_weight, preferred_element_type=...  16.1 us
    all_gather x1, blocking collectives, shards(): block_rows = lax.all_gather(own_block, 'ffn', axis=1, tiled=True)  15.6 us
    all_gather x1, blocking collectives, shards(): lax.all_gather(join_parts(parts, group_heads), 'ffn', axis=0, tiled=True)  14.6 us
    all_to_all x1, blocking collectives, scatter_sum(): parts = lax.all_to_all(half, 'ffn', 0, 0, axis_index_groups=chips)  14.1 us
    all_to_all x1, waiting for transfers between devices, scatter_sum(): parts = lax.all_to_all(half, 'ffn', 0, 0, axis_index_groups=chips)  12.8 us
  transfers between devices with their start and end apart: 3, of which 3 were waited for; matrix products, arithmetic and copies ran while one was open for 2% of the time, Pallas kernels for 0%

profile of v2, /device:TPU:0, one launch (start us, length us, event | category | flops | bytes accessed | tf_op | source)
XLA Modules:
  0.0 229.0 jit_solution(7711009939604258965)
XLA Ops:
  6.5 0.0 copy-start
  6.5 1.3 fusion.14
  7.8 1.8 convolution_convert_fusion.2
  9.6 0.0 copy-done.2
  9.6 0.0 copy-done.6
  9.6 1.6 convolution_convert_fusion.3
  11.2 1.6 convolution_convert_fusion.4
  12.9 0.1 broadcast_in_dim.115
  13.0 0.1 pad_maximum_fusion
  13.2 0.9 reshape.185
  14.1 0.4 copy.70
  14.5 4.7 %all_to_all.30 = bf16[2,4,288,256]{3,1,2,0:T(4,128)(2,1)S(1)} all-to-all(bf16[2,4,288,256]{3,1,2,0:T(4,128)(2,1)S(1)} %bitcast.82), channel_id=1, replica_groups={{0,1},{2,3},{4,5},{6,7},{8,9},{10,11},{12,13},{14,15},{16,17},{18,19},{..., dimensions={0} | all-to-all | bytes 2359296 | tf_op jit(solution)/shard_map/all_to_all | solution.py:57
  19.2 1.2 reduce_sum.151
  20.4 0.9 copy.48
  21.3 6.3 %all-to-all-start.1 = ((bf16[4,288,256]{2,1,0:T(8,128)(2,1)}), bf16[4,288,256]{2,1,0:T(8,128)(2,1)S(1)}, u32[]{:S(2)}, u32[]{:S(2)}) async-start(bf16[4,288,256]{2,1,0:T(8,128)(2,1)} %copy.48), calls=%async_computation.1 | async-start | bytes 1179648 | tf_op jit(solution)/shard_map/all_to_all | solution.py:59
  27.6 0.0 all-gather.5.cloned.1.call-start
  27.7 0.0 copy-done.4
  27.7 0.4 select_reduce_fusion
  28.1 0.0 copy-done.5
  28.1 0.1 pad_add_fusion.1
  28.2 0.1 select_reduce_fusion.4
  28.3 0.1 convert_reduce_fusion.3
  28.5 0.7 fusion.41
  31.0 0.1 add_bitcast_fusion
  31.1 12.8 %all-to-all-done.1 = bf16[4,288,256]{2,1,0:T(8,128)(2,1)S(1)} async-done(((bf16[4,288,256]{2,1,0:T(8,128)(2,1)}), bf16[4,288,256]{2,1,0:T(8,128)(2,1)S(1)}, u32[]{:S(2)}, u32[]{:S(2)}) %all-to-all-start.1) | async-done | bytes 589856 | tf_op jit(solution)/shard_map/all_to_all | solution.py:59
  43.8 0.1 reduce_sum.152
  43.9 17.2 %all-gather = bf16[1152,256]{1,0:T(8,128)(2,1)} all-gather(bf16[288,256]{1,0:T(8,128)(2,1)S(1)} %reduce_sum.152), channel_id=2, replica_groups={{0,2,4,6},{1,3,5,7},{8,10,12,14},{9,11,13,15},{16,18,20,22},{17,19,21,2..., dimensions={0}, use_global_device_ids=true | all-gather | bytes 737280 | tf_op jit(solution)/shard_map/all_gather | solution.py:434
  61.1 0.0 all-gather.5.cloned.1.call-update
  61.1 0.7 pad_add_fusion.2
  61.9 0.2 convert_reduce_fusion.2
  62.0 0.6 compare_select_fusion.2
  62.7 0.1 select_reduce_fusion.3
  62.9 0.6 fusion.30
  63.5 0.1 pad_maximum_fusion.1
  63.6 5.5 %all-gather.5.cloned.1.call-done = bf16[8,288,256]{2,1,0:T(8,128)(2,1)} async-done(((bf16[4,288,256]{2,1,0:T(8,128)(2,1)}), bf16[8,288,256]{2,1,0:T(8,128)(2,1)}) %all-gather.5.cloned.1.call-update) | async-done | bytes 1179664 | tf_op jit(solution)/shard_map/all_gather | solution.py:435
  69.1 3.2 %copy.69 = bf16[2,4,288,256]{3,1,0,2:T(4,128)(2,1)} copy(bf16[2,4,288,256]{3,2,1,0:T(8,128)(2,1)} %bitcast.86) | data formatting | bytes 2359296 | tf_op jit(solution)/shard_map/all_gather | solution.py:435
  72.3 2.6 %reshape.186.reduced = bf16[288,2048]{1,0:T(8,128)(2,1)S(1)} reshape(bf16[288,2,4,256]{3,2,1,0:T(4,128)(2,1)} %bitcast.83) | data formatting | bytes 2359296 | tf_op jit(solution)/shard_map/reshape | solution.py:436
  74.9 37.1 %paged_attention.1 = (bf16[256,768]{1,0:T(8,128)(2,1)S(1)}, f32[32,8,128]{2,1,0:T(8,128)S(1)}, f32[32,8,128]{2,1,0:T(8,128)S(1)}) custom-call(s32[4,128]{1,0:T(4,128)S(1)} %pad_add_fusion.plan, bf16[288,2048]{1,0:T(8,128)(2,1)S(1)} %reshape.186.reduced, f32[288,128]{1,0:T(8,128)S(1)} %get-tuple-element.26.cosine, f32[288,128]{1,0:T(8,128)S(1)} %get-tuple-element.27.sine, ...), custom_call_target="tpu_custom_call" | custom-call | tf_op jit(solution)/shard_map/paged_attention/pallas_call | solution.py:299
  112.1 0.1 reshape.199
  112.2 0.1 reshape.189
  112.3 19.9 %all_to_all.31 = bf16[8,36,768]{2,1,0:T(8,128)(2,1)S(1)} all-to-all(bf16[8,36,768]{2,1,0:T(8,128)(2,1)S(1)} %reshape.189), channel_id=1, replica_groups=mesh['grp'=4,'ffn'=8] {'ffn'}, dimensions={0} | all-to-all | bytes 884736 | tf_op jit(solution)/shard_map/all_to_all | solution.py:438
  132.2 0.1 copy.52
  132.4 0.1 copy.53
  132.6 0.3 broadcast_bitcast_fusion
  132.8 0.1 copy.55
  132.9 0.1 div.53
  133.1 0.1 convert_element_type.92
  133.2 0.2 fusion.6
  133.4 14.6 %all-gather.2 = bf16[8,36,640]{2,1,0:T(8,128)(2,1)S(1)} all-gather(bf16[1,36,640]{2,1,0:T(8,128)(2,1)S(1)} %fusion.29), channel_id=1, replica_groups=mesh['grp'=4,'ffn'=8] {'ffn'}, dimensions={0}, use_global_device_ids=true | all-gather | bytes 414720 | tf_op jit(solution)/shard_map/all_gather | solution.py:441
  148.0 0.1 reshape.197
  148.0 1.2 convolution_convert_fusion.1
  149.3 3.8 %all-to-all-start.3 = ((bf16[4,72,640]{2,1,0:T(8,128)(2,1)}), bf16[4,72,640]{2,1,0:T(8,128)(2,1)S(1)}, u32[]{:S(2)}, u32[]{:S(2)}) async-start(bf16[4,72,640]{2,1,0:T(8,128)(2,1)} %bitcast.25), calls=%async_computation.3 | async-start | bytes 737280 | tf_op jit(solution)/shard_map/all_to_all | solution.py:444
  153.1 6.9 %all-to-all-done.3 = bf16[4,72,640]{2,1,0:T(8,128)(2,1)S(1)} async-done(((bf16[4,72,640]{2,1,0:T(8,128)(2,1)}), bf16[4,72,640]{2,1,0:T(8,128)(2,1)S(1)}, u32[]{:S(2)}, u32[]{:S(2)}) %all-to-all-start.3) | async-done | bytes 368672 | tf_op jit(solution)/shard_map/all_to_all | solution.py:444
  160.1 15.6 %all_gather.23 = bf16[72,5120]{1,0:T(8,128)(2,1)S(1)} all-gather(bf16[72,640]{1,0:T(8,128)(2,1)S(1)} %add_convert_fusion.1), channel_id=1, replica_groups=mesh['grp'=4,'ffn'=8] {'ffn'}, dimensions={1}, use_global_device_ids=true | all-gather | bytes 829440 | tf_op jit(solution)/shard_map/all_gather | solution.py:451
  175.6 0.3 fusion
  175.9 16.1 %convolution_bitcast_fusion = f32[2,72,1728]{2,1,0:T(8,128)S(1)} fusion(bf16[2,5120,1728]{1,2,0:T(8,128)(2,1)} %param.19, bf16[72,5120]{1,0:T(8,128)(2,1)S(1)} %all_gather.23, f32[5120]{0:T(1024)S(1)} %copy-done.3, f32[72]{0:T(128)S(1)} %add_rsqrt_fusion), kind=kOutput, calls=%fused_computation.1 | convolution fusion | flops 2549514240 | bytes 37142816 | tf_op jit(solution)/shard_map/td,kdf->ktf/dot_general | solution.py:455
  192.0 9.2 %convolution_convert_fusion = bf16[72,5120]{1,0:T(8,128)(2,1)S(1)} fusion(bf16[1728,5120]{1,0:T(8,128)(2,1)} %param.20, f32[2,72,1728]{2,1,0:T(8,128)S(1)} %convolution_bitcast_fusion), kind=kOutput, calls=%fused_computation | convolution fusion | flops 1275134976 | bytes 19427328 | tf_op jit(solution)/shard_map/dot_general | solution.py:457
  201.2 0.6 reshape.192
  201.8 0.3 copy.71
  202.1 0.0 copy-start.1
  202.1 4.4 %all_to_all.32 = bf16[2,4,72,640]{3,1,2,0:T(4,128)(2,1)S(1)} all-to-all(bf16[2,4,72,640]{3,1,2,0:T(4,128)(2,1)S(1)} %bitcast.84), channel_id=1, replica_groups={{0,1},{2,3},{4,5},{6,7},{8,9},{10,11},{12,13},{14,15},{16,17},{18,19},{..., dimensions={0} | all-to-all | bytes 1474560 | tf_op jit(solution)/shard_map/all_to_all | solution.py:57
  206.5 0.7 reduce_sum.157
  207.3 14.1 %all_to_all.33 = bf16[4,72,640]{2,1,0:T(8,128)(2,1)S(1)} all-to-all(bf16[4,72,640]{2,1,0:T(8,128)(2,1)S(1)} %copy.58), channel_id=1, replica_groups={{0,2,4,6},{1,3,5,7},{8,10,12,14},{9,11,13,15},{16,18,20,22},{17,19,21,2..., dimensions={0} | all-to-all | bytes 737280 | tf_op jit(solution)/shard_map/all_to_all | solution.py:59
  221.5 0.7 add_convert_fusion
  (35 shorter events, 0.5 us)
Async XLA Ops:
  6.5 141.5 %copy-start = (bf16[640,640]{1,0:T(8,128)(2,1)S(1)}, bf16[640,640]{1,0:T(8,128)(2,1)}, u32[]{:S(2)}) copy-start(bf16[640,640]{1,0:T(8,128)(2,1)} %param.17) | copy-start | bytes 2457604
  6.5 3.0 %copy-start.2 = (bf16[288,640]{1,0:T(8,128)(2,1)S(1)}, bf16[288,640]{1,0:T(8,128)(2,1)}, u32[]{:S(2)}) copy-start(bf16[288,640]{1,0:T(8,128)(2,1)} %param.12) | copy-start | bytes 1105924
  6.5 3.0 %copy-start.6 = (f32[640]{0:T(1024)S(1)}, f32[640]{0:T(1024)}, u32[]{:S(2)}) copy-start(f32[640]{0:T(1024)} %param.13) | copy-start | bytes 7684
  19.2 8.5 %copy-start.4 = (s32[34,128]{1,0:T(8,128)S(1)}, s32[34,128]{1,0:T(8,128)}, u32[]{:S(2)}) copy-start(s32[34,128]{1,0:T(8,128)} %param.23) | copy-start | bytes 52228
  19.2 8.9 %copy-start.5 = (s32[32]{0:T(128)S(1)}, s32[32]{0:T(128)}, u32[]{:S(2)}) copy-start(s32[32]{0:T(128)} %param.22) | copy-start | bytes 388
  19.2 8.9 %copy-start.7 = (s32[2]{0:T(128)S(1)}, s32[2]{0:T(128)}, u32[]{:S(2)}) copy-start(s32[2]{0:T(128)} %param.21) | copy-start | bytes 28
  21.3 22.5 %all-to-all-start.1 = ((bf16[4,288,256]{2,1,0:T(8,128)(2,1)}), bf16[4,288,256]{2,1,0:T(8,128)(2,1)S(1)}, u32[]{:S(2)}, u32[]{:S(2)}) async-start(bf16[4,288,256]{2,1,0:T(8,128)(2,1)} %copy.48), calls=%async_computation.1 | async-start | bytes 1179648 | tf_op jit(solution)/shard_map/all_to_all | solution.py:59
  27.6 41.5 %all-gather.5.cloned.1.call-start = ((), (), s32[]{:S(2)}) async-start(), calls=%async_computation.6 | async-start | bytes 1769472 | tf_op jit(solution)/shard_map/all_gather | solution.py:435
  149.3 26.6 %copy-start.3 = (f32[5120]{0:T(1024)S(1)}, f32[5120]{0:T(1024)}, u32[]{:S(2)}) copy-start(f32[5120]{0:T(1024)} %param.18) | copy-start | bytes 61444
  149.3 10.7 %all-to-all-start.3 = ((bf16[4,72,640]{2,1,0:T(8,128)(2,1)}), bf16[4,72,640]{2,1,0:T(8,128)(2,1)S(1)}, u32[]{:S(2)}, u32[]{:S(2)}) async-start(bf16[4,72,640]{2,1,0:T(8,128)(2,1)} %bitcast.25), calls=%async_computation.3 | async-start | bytes 737280 | tf_op jit(solution)/shard_map/all_to_all | solution.py:444
  202.1 20.1 %copy-start.1 = (bf16[640,640]{1,0:T(8,128)(2,1)S(1)}, bf16[640,640]{1,0:T(8,128)(2,1)}, u32[]{:S(2)}) copy-start(bf16[640,640]{1,0:T(8,128)(2,1)} %param.17) | copy-start | bytes 2457604
Sparse Core Ops, SparseCore 0:
  61.3 7.7 all-gather.4

commit v3 on v2

--- a/solution.py
+++ b/solution.py
@@ -58,6 +58,14 @@
     half = jnp.sum(halves.astype(jnp.float32), axis=0).astype(blocks.dtype)
     parts = lax.all_to_all(half, "ffn", 0, 0, axis_index_groups=chips)
     return jnp.sum(parts.astype(jnp.float32), axis=0)
+
+
+def gather_all(block):
+    n = lax.axis_size("ffn")
+    mine = lax.all_gather(block, "ffn", axis_index_groups=pair_groups(n)[1])
+    other = lax.ppermute(mine, "ffn", [(i, i ^ 1) for i in range(n)])
+    even = lax.axis_index("ffn") % 2 == 0
+    return jnp.stack([jnp.where(even, mine, other), jnp.where(even, other, mine)])
 
 
 def split_bf16(value, pieces):
@@ -127,12 +135,17 @@
     run_o[...] = jnp.zeros_like(run_o)
 
     width = heads * HD
-    squares = reduced[:, 3 * width : 3 * width + HD].astype(jnp.float32)
+    block = reduced.shape[2]
+
+    def lanes_at(start):
+        offset = start % block
+        return reduced[start // block, :, offset : offset + HD].astype(jnp.float32)
+
+    squares = lanes_at(3 * width)
     inverse = lax.rsqrt(squares / D + EPS)
 
     def projected(which, head):
-        start = which * width + head * HD
-        return reduced[:, start : start + HD].astype(jnp.float32) * inverse
+        return lanes_at(which * width + head * HD) * inverse
 
     def turned(value):
         swapped = jnp.concatenate([value[:, HD // 2 :], value[:, : HD // 2]], axis=1)
@@ -426,19 +439,25 @@
         + [jnp.broadcast_to(squares[:, None], (TOKENS, HD)).astype(jnp.bfloat16)],
         axis=1,
     )
-    pairs, chips = pair_groups(n_ffn)
     columns = partial_value.shape[1] // n_ffn
     own_sum = scatter_sum(
         partial_value.reshape(TOKENS, 2, n_ffn // 2, columns).transpose(1, 2, 0, 3)
     ).astype(jnp.bfloat16)
-    of_core = lax.all_gather(own_sum, "ffn", axis_index_groups=chips)
-    gathered = lax.all_gather(of_core, "ffn", axis_index_groups=pairs)
-    reduced = gathered.transpose(2, 0, 1, 3).reshape(partial_value.shape)
+    gathered = gather_all(own_sum)
+    if columns % HD == 0:
+        reduced = gathered.reshape(n_ffn, TOKENS, columns)
+    else:
+        reduced = gathered.transpose(2, 0, 1, 3).reshape(1, TOKENS, n_ffn * columns)
     packed = attention(plan, reduced, positions, key_cache, value_cache)
     parts = lax.all_to_all(
-        packed.reshape(n_ffn, TOKENS // n_ffn, packed.shape[1]), "ffn", 0, 0
-    )
-    heads_out = lax.all_gather(join_parts(parts, group_heads), "ffn", axis=0, tiled=True)
+        packed.reshape(2, n_ffn // 2, TOKENS // n_ffn, packed.shape[1])
+        .swapaxes(0, 1)
+        .reshape(n_ffn, TOKENS // n_ffn, packed.shape[1]),
+        "ffn",
+        0,
+        0,
+    )
+    heads_out = gather_all(join_parts(parts, group_heads)).reshape(TOKENS, group_width)
     head_part = jnp.dot(heads_out, out_weight, preferred_element_type=jnp.float32)
     quarter = TOKENS // n_grp
     blocks = lax.all_to_all(
@@ -448,7 +467,7 @@
     own_block = (
         own_input.astype(jnp.float32) + jnp.sum(blocks.astype(jnp.float32), axis=0)
     ).astype(jnp.bfloat16)
-    block_rows = lax.all_gather(own_block, "ffn", axis=1, tiled=True)
+    block_rows = gather_all(own_block).transpose(2, 1, 0, 3).reshape(quarter, D)
     rows_f32 = block_rows.astype(jnp.float32)
     inverse = lax.rsqrt(jnp.sum(rows_f32 * rows_f32, axis=1) / D + EPS)[:, None]
     normed = (rows_f32 * inverse * ffn_gain[None, :]).astype(jnp.bfloat16)

time: 229 us -> 218 us (0.952)
  between operations: 15.6 us -> 2.22 us
  other arithmetic: 8.12 us -> 13.6 us
  local copies, waits for them, and re-layouts: 10.8 us -> 13.9 us
  blocking collectives: 90.5 us -> 87.6 us
  waiting for transfers between devices: 25.2 us -> 22.3 us
    all_gather x1 -> x0, waiting for transfers between devices: 5.5 us -> none  [shards(): gathered = lax.all_gather(of_core, 'ffn', axis_index_groups=pairs)]
    convert_element_type x0 -> x3, local copies, waits for them, and re-layouts: none -> 4.92 us  [the longest x2 4.78 us: shards(): rows_f32 = block_rows.astype(jnp.float32)]
    ppermute x0 -> x3, waiting for transfers between devices: none -> 4.22 us  [gather_all(): other = lax.ppermute(mine, 'ffn', [(i, i ^ 1) for i in range(n)])]
    all_gather x1 -> x0, local copies, waits for them, and re-layouts: 3.23 us -> none  [shards(): gathered = lax.all_gather(of_core, 'ffn', axis_index_groups=pairs)]
    mul x2 -> x3, local copies, waits for them, and re-layouts: 0.39 us -> 3.54 us  [join_parts(): outs * share[..., None]]
    reshape x2 -> x3, local copies, waits for them, and re-layouts: 2.69 us -> 0.19 us  [the longest x1 0.09 us: shards(): packed.reshape(2, n_ffn // 2, TOKENS // n_ffn, packed.shape[1])]
    reduce_sum x1, other arithmetic: 0.15 us -> 2.6 us  [join_parts(): jnp.sum(outs * share[..., None], axis=0) / jnp.sum(share, axis=0)[..., None]]
  transfers between devices with their start and end apart: 3 -> 5, of which waited for: 3 -> 5; matrix products, arithmetic and copies ran while one was open for 2% -> 2% of each run, Pallas kernels for 0% -> 0%
where the time goes in v3:
time: 218 us; the launch traced here: 220 us
  blocking collectives  87.6 us (40%)
  Pallas kernels  38.9 us (18%)
  matrix products  31.6 us (14%)
  waiting for transfers between devices  22.3 us (10%)
  local copies, waits for them, and re-layouts  13.9 us (6%)
  other arithmetic  13.6 us (6%)
  starting transfers between devices  10 us (5%)
  between operations  2.22 us (1%)
    all_gather x3, blocking collectives, gather_all(): mine = lax.all_gather(block, 'ffn', axis_index_groups=pair_groups(n)[1])  45.3 us
    pallas_call x1, Pallas kernels, attention(): pl.pallas_call(functools.partial(attention_kernel, heads), out_shape=(jax...  38.9 us
    all_to_all x1, blocking collectives, shards(): lax.all_to_all(packed.reshape(2, n_ffn // 2, TOKENS // n_ffn, packed.shap...  19.1 us
    dot_general x1, matrix products, shards(): jnp.einsum('td,kdf->ktf', normed, gate_up_weight, preferred_element_type=...  16.1 us
    all_to_all x1, blocking collectives, scatter_sum(): parts = lax.all_to_all(half, 'ffn', 0, 0, axis_index_groups=chips)  14.1 us
    all_to_all x1, waiting for transfers between devices, scatter_sum(): parts = lax.all_to_all(half, 'ffn', 0, 0, axis_index_groups=chips)  11.4 us
    dot_general x1, matrix products, shards(): jnp.dot(hidden, down_weight, preferred_element_type=jnp.float32)  9.24 us
    all_to_all x2, blocking collectives, scatter_sum(): halves = lax.all_to_all(blocks, 'ffn', 0, 0, axis_index_groups=pairs)  9.11 us
  transfers between devices with their start and end apart: 5, of which 5 were waited for; matrix products, arithmetic and copies ran while one was open for 2% of the time, Pallas kernels for 0%

profile of v3, /device:TPU:0, one launch (start us, length us, event | category | flops | bytes accessed | tf_op | source)
XLA Modules:
  0.0 220.1 jit_solution(18067183324699173303)
XLA Ops:
  0.0 1.3 fusion.12
  1.3 1.8 convolution_convert_fusion.3
  3.1 1.6 convolution_convert_fusion.2
  4.7 1.6 convolution_convert_fusion.4
  6.4 0.1 broadcast_in_dim.115
  6.5 0.2 pad_maximum_fusion
  6.6 0.9 reshape.210
  7.6 0.4 copy.81
  8.0 4.7 %all_to_all.30 = bf16[2,4,288,256]{3,1,2,0:T(4,128)(2,1)S(1)} all-to-all(bf16[2,4,288,256]{3,1,2,0:T(4,128)(2,1)S(1)} %bitcast.98), channel_id=1, replica_groups={{0,1},{2,3},{4,5},{6,7},{8,9},{10,11},{12,13},{14,15},{16,17},{18,19},{..., dimensions={0} | all-to-all | bytes 2359296 | tf_op jit(solution)/shard_map/all_to_all | solution.py:57
  12.7 1.2 reduce_sum.153
  13.9 0.9 copy.55
  14.8 6.3 %all-to-all-start.1 = ((bf16[4,288,256]{2,1,0:T(8,128)(2,1)}), bf16[4,288,256]{2,1,0:T(8,128)(2,1)S(1)}, u32[]{:S(2)}, u32[]{:S(2)}) async-start(bf16[4,288,256]{2,1,0:T(8,128)(2,1)} %copy.55), calls=%async_computation.1 | async-start | bytes 1179648 | tf_op jit(solution)/shard_map/all_to_all | solution.py:59
  21.2 0.4 select_reduce_fusion
  21.6 0.1 pad_add_fusion.1
  21.7 0.1 select_reduce_fusion.4
  21.8 0.1 convert_reduce_fusion.3
  21.9 0.7 fusion.39
  24.4 0.6 pad_add_fusion.2
  25.1 0.1 add_bitcast_fusion
  25.1 0.2 convert_reduce_fusion.2
  25.3 0.6 compare_select_fusion.2
  25.9 11.4 %all-to-all-done.1 = bf16[4,288,256]{2,1,0:T(8,128)(2,1)S(1)} async-done(((bf16[4,288,256]{2,1,0:T(8,128)(2,1)}), bf16[4,288,256]{2,1,0:T(8,128)(2,1)S(1)}, u32[]{:S(2)}, u32[]{:S(2)}) %all-to-all-start.1) | async-done | bytes 589856 | tf_op jit(solution)/shard_map/all_to_all | solution.py:59
  37.3 0.1 reduce_sum.154
  37.4 16.4 %all-gather = bf16[1152,256]{1,0:T(8,128)(2,1)S(1)} all-gather(bf16[288,256]{1,0:T(8,128)(2,1)S(1)} %reduce_sum.154), channel_id=2, replica_groups={{0,2,4,6},{1,3,5,7},{8,10,12,14},{9,11,13,15},{16,18,20,22},{17,19,21,2..., dimensions={0}, use_global_device_ids=true | all-gather | bytes 737280 | tf_op jit(solution)/shard_map/all_gather | solution.py:65
  53.9 0.1 select_reduce_fusion.3
  54.0 0.6 fusion.28
  54.6 0.1 pad_maximum_fusion.4
  54.8 1.1 collective-permute-done
  55.8 0.1 select_bitcast_fusion.1
  55.9 0.1 pad_maximum_fusion.1
  56.1 38.9 %paged_attention.1 = (bf16[256,768]{1,0:T(8,128)(2,1)S(1)}, f32[32,8,128]{2,1,0:T(8,128)S(1)}, f32[32,8,128]{2,1,0:T(8,128)S(1)}) custom-call(s32[4,128]{1,0:T(4,128)S(1)} %pad_add_fusion.plan, bf16[8,288,256]{2,1,0:T(8,128)(2,1)S(1)} %bitcast.97, f32[288,128]{1,0:T(8,128)S(1)} %get-tuple-element.32.cosine, f32[288,128]{1,0:T(8,128)S(1)} %get-tuple-element.33.sine, ...), custom_call_target="tpu_custom_call" | custom-call | tf_op jit(solution)/shard_map/paged_attention/pallas_call | solution.py:312
  95.0 0.1 reshape.225
  95.1 0.1 reshape.214
  95.3 19.1 %all_to_all.31 = bf16[8,36,768]{2,1,0:T(8,128)(2,1)S(1)} all-to-all(bf16[8,36,768]{2,1,0:T(8,128)(2,1)S(1)} %bitcast.103), channel_id=1, replica_groups=mesh['grp'=4,'ffn'=8] {'ffn'}, dimensions={0} | all-to-all | bytes 884736 | tf_op jit(solution)/shard_map/all_to_all | solution.py:452
  114.3 1.2 copy.60
  115.6 1.9 convert_element_type.108
  117.5 0.1 copy.61
  117.6 1.1 broadcast_bitcast_fusion
  118.7 2.3 %copy.62 = f32[8,36,640]{1,0,2:T(8,128)S(1)} copy(f32[8,36,640]{2,0,1:T(8,128)} %broadcast_bitcast_fusion) | data formatting | bytes 1474560 | tf_op jit(solution)/shard_map/mul | solution.py:399
  121.0 2.6 %fusion = f32[36,640]{0,1:T(8,128)S(1)} fusion(f32[8,36,640]{1,0,2:T(8,128)S(1)} %copy.62, f32[8,36,768]{1,0,2:T(8,128)} %convert_element_type.108), kind=kLoop, calls=%fused_computation.2 | loop fusion | flops 345600 | bytes 1566720 | tf_op jit(solution)/shard_map/reduce_sum | solution.py:399
  123.7 0.1 copy.65
  123.8 13.9 %all_gather.17 = bf16[4,36,640]{2,1,0:T(8,128)(2,1)S(1)} all-gather(bf16[1,36,640]{2,1,0:T(8,128)(2,1)S(1)} %copy.65), channel_id=1, replica_groups={{0,2,4,6},{1,3,5,7},{8,10,12,14},{9,11,13,15},{16,18,20,22},{17,19,21,2..., dimensions={0}, use_global_device_ids=true | all-gather | bytes 230400 | tf_op jit(solution)/shard_map/all_gather | solution.py:65
  137.7 1.5 collective-permute-done.1
  139.2 0.1 pad_maximum_fusion.3
  139.2 0.1 reshape.217
  139.3 1.2 convolution_convert_fusion.1
  140.6 3.7 %all-to-all-start.3 = ((bf16[4,72,640]{2,1,0:T(8,128)(2,1)}), bf16[4,72,640]{2,1,0:T(8,128)(2,1)S(1)}, u32[]{:S(2)}, u32[]{:S(2)}) async-start(bf16[4,72,640]{2,1,0:T(8,128)(2,1)} %bitcast.31), calls=%async_computation.3 | async-start | bytes 737280 | tf_op jit(solution)/shard_map/all_to_all | solution.py:463
  144.3 6.7 %all-to-all-done.3 = bf16[4,72,640]{2,1,0:T(8,128)(2,1)S(1)} async-done(((bf16[4,72,640]{2,1,0:T(8,128)(2,1)}), bf16[4,72,640]{2,1,0:T(8,128)(2,1)S(1)}, u32[]{:S(2)}, u32[]{:S(2)}) %all-to-all-start.3) | async-done | bytes 368672 | tf_op jit(solution)/shard_map/all_to_all | solution.py:463
  151.0 0.9 add_convert_fusion.1
  151.9 15.0 %all-gather.1 = bf16[288,640]{1,0:T(8,128)(2,1)S(1)} all-gather(bf16[72,640]{1,0:T(8,128)(2,1)S(1)} %add_convert_fusion.1), channel_id=3, replica_groups={{0,2,4,6},{1,3,5,7},{8,10,12,14},{9,11,13,15},{16,18,20,22},{17,19,21,2..., dimensions={0}, use_global_device_ids=true | all-gather | bytes 460800 | tf_op jit(solution)/shard_map/all_gather | solution.py:65
  166.9 1.7 collective-permute-done.2
  168.6 0.1 select_bitcast_fusion.3
  168.7 0.3 fusion.1
  168.9 0.1 convert_bitcast_fusion
  169.0 2.3 %copy.66 = f32[72,4,2,640]{3,2,1,0:T(2,128)} copy(f32[72,4,2,640]{3,0,1,2:T(8,128)S(1)} %convert_bitcast_fusion) | data formatting | bytes 2949120 | tf_op jit(solution)/shard_map/convert_element_type | solution.py:471
  171.3 2.5 %reshape.221 = f32[72,5120]{1,0:T(8,128)S(1)} reshape(f32[72,4,2,640]{3,2,1,0:T(2,128)} %copy.66) | data formatting | bytes 2949120 | tf_op jit(solution)/shard_map/convert_element_type | solution.py:471
  173.8 16.1 %convolution_bitcast_fusion = f32[2,72,1728]{2,1,0:T(8,128)S(1)} fusion(bf16[2,5120,1728]{1,2,0:T(8,128)(2,1)} %param.19, f32[72,5120]{1,0:T(8,128)S(1)} %reshape.221, f32[5120]{0:T(1024)S(1)} %copy-done.3, f32[72]{0:T(128)S(1)} %add_rsqrt_fusion), kind=kOutput, calls=%fused_computation.3 | convolution fusion | flops 2549145600 | bytes 37880096 | tf_op jit(solution)/shard_map/td,kdf->ktf/dot_general | solution.py:474
  189.9 9.2 %convolution_convert_fusion = bf16[72,5120]{1,0:T(8,128)(2,1)S(1)} fusion(bf16[1728,5120]{1,0:T(8,128)(2,1)} %param.20, f32[2,72,1728]{2,1,0:T(8,128)S(1)} %convolution_bitcast_fusion), kind=kOutput, calls=%fused_computation | convolution fusion | flops 1275134976 | bytes 19427328 | tf_op jit(solution)/shard_map/dot_general | solution.py:476
  199.2 0.6 reshape.219
  199.8 0.3 copy.82
  200.1 4.4 %all_to_all.32 = bf16[2,4,72,640]{3,1,2,0:T(4,128)(2,1)S(1)} all-to-all(bf16[2,4,72,640]{3,1,2,0:T(4,128)(2,1)S(1)} %bitcast.99), channel_id=1, replica_groups={{0,1},{2,3},{4,5},{6,7},{8,9},{10,11},{12,13},{14,15},{16,17},{18,19},{..., dimensions={0} | all-to-all | bytes 1474560 | tf_op jit(solution)/shard_map/all_to_all | solution.py:57
  204.5 0.7 reduce_sum.160
  205.3 14.1 %all_to_all.33 = bf16[4,72,640]{2,1,0:T(8,128)(2,1)S(1)} all-to-all(bf16[4,72,640]{2,1,0:T(8,128)(2,1)S(1)} %copy.69), channel_id=1, replica_groups={{0,2,4,6},{1,3,5,7},{8,10,12,14},{9,11,13,15},{16,18,20,22},{17,19,21,2..., dimensions={0} | all-to-all | bytes 737280 | tf_op jit(solution)/shard_map/all_to_all | solution.py:59
  219.5 0.7 add_convert_fusion
  (43 shorter events, 0.5 us)
Async XLA Ops:
  0.0 139.3 %copy-start = (bf16[640,640]{1,0:T(8,128)(2,1)S(1)}, bf16[640,640]{1,0:T(8,128)(2,1)}, u32[]{:S(2)}) copy-start(bf16[640,640]{1,0:T(8,128)(2,1)} %param.17) | copy-start | bytes 2457604
  0.0 3.0 %copy-start.2 = (bf16[288,640]{1,0:T(8,128)(2,1)S(1)}, bf16[288,640]{1,0:T(8,128)(2,1)}, u32[]{:S(2)}) copy-start(bf16[288,640]{1,0:T(8,128)(2,1)} %param.12) | copy-start | bytes 1105924
  0.0 3.0 %copy-start.6 = (f32[640]{0:T(1024)S(1)}, f32[640]{0:T(1024)}, u32[]{:S(2)}) copy-start(f32[640]{0:T(1024)} %param.13) | copy-start | bytes 7684
  12.7 8.5 %copy-start.4 = (s32[34,128]{1,0:T(8,128)S(1)}, s32[34,128]{1,0:T(8,128)}, u32[]{:S(2)}) copy-start(s32[34,128]{1,0:T(8,128)} %param.23) | copy-start | bytes 52228
  12.7 8.9 %copy-start.5 = (s32[32]{0:T(128)S(1)}, s32[32]{0:T(128)}, u32[]{:S(2)}) copy-start(s32[32]{0:T(128)} %param.22) | copy-start | bytes 388
  12.7 8.9 %copy-start.7 = (s32[2]{0:T(128)S(1)}, s32[2]{0:T(128)}, u32[]{:S(2)}) copy-start(s32[2]{0:T(128)} %param.21) | copy-start | bytes 28
  14.8 22.5 %all-to-all-start.1 = ((bf16[4,288,256]{2,1,0:T(8,128)(2,1)}), bf16[4,288,256]{2,1,0:T(8,128)(2,1)S(1)}, u32[]{:S(2)}, u32[]{:S(2)}) async-start(bf16[4,288,256]{2,1,0:T(8,128)(2,1)} %copy.55), calls=%async_computation.1 | async-start | bytes 1179648 | tf_op jit(solution)/shard_map/all_to_all | solution.py:59
  53.8 2.0 collective-permute-start
  137.7 1.5 collective-permute-start.1
  140.6 10.4 %all-to-all-start.3 = ((bf16[4,72,640]{2,1,0:T(8,128)(2,1)}), bf16[4,72,640]{2,1,0:T(8,128)(2,1)S(1)}, u32[]{:S(2)}, u32[]{:S(2)}) async-start(bf16[4,72,640]{2,1,0:T(8,128)(2,1)} %bitcast.31), calls=%async_computation.3 | async-start | bytes 737280 | tf_op jit(solution)/shard_map/all_to_all | solution.py:463
  166.9 1.7 collective-permute-start.2
  171.3 2.5 %copy-start.3 = (f32[5120]{0:T(1024)S(1)}, f32[5120]{0:T(1024)}, u32[]{:S(2)}) copy-start(f32[5120]{0:T(1024)} %param.18) | copy-start | bytes 61444
  200.0 20.1 %copy-start.1 = (bf16[640,640]{1,0:T(8,128)(2,1)S(1)}, bf16[640,640]{1,0:T(8,128)(2,1)}, u32[]{:S(2)}) copy-start(bf16[640,640]{1,0:T(8,128)(2,1)} %param.17) | copy-start | bytes 2457604
